TPU v7x, 32 devices: a whole 2x2x4 slice. The times are simulated.
32 devices in a mesh: dp: 4 (over z), col: 8 (over y, x, core).
Axes of the slice: x: 2, y: 2, z: 4, core: 2. Of those that a mesh axis runs over, the one named last changes fastest.
Arguments:
- inputs: bfloat16 [4096, 768], P(('dp', 'col')), may hold values from -6 to 6
- gain_one: float32 [768], replicated, may hold values from 0.5 to 1.5
- shift_one: float32 [768], replicated, may hold values from -1.25 to 1.25
- w_qkv: bfloat16 [768, 2304], replicated, may hold values from -0.21875 to 0.21875
- bias_q: float32 [768], replicated, may hold values from -1.25 to 1.25
- bias_v: float32 [768], replicated, may hold values from -0.1875 to 0.1875
- w_out: bfloat16 [768, 768], replicated, may hold values from -3 to 3
- bias_out: float32 [768], replicated, may hold values from -1.25 to 1.25
- gain_two: float32 [768], replicated, may hold values from 0.5 to 1.5
- shift_two: float32 [768], replicated, may hold values from -1.25 to 1.25
- w_up: bfloat16 [768, 3072], replicated, may hold values from -0.21875 to 0.21875
- bias_up: float32 [3072], replicated, may hold values from -1.25 to 1.25
- w_down: bfloat16 [3072, 768], replicated, may hold values from -0.109375 to 0.109375
- bias_down: float32 [768], replicated, may hold values from -1.25 to 1.25
- lengths: int32 [4, 4], P('dp'), may hold values from 1 to 960, 1024 in all within a row
- cotangent: bfloat16 [4096, 768], P(('dp', 'col')), may hold values from -6 to 6
Outputs:
- layer_out: bfloat16 [4096, 768], P(('dp', 'col'))
- grad_inputs: bfloat16 [4096, 768], P(('dp', 'col'))
- grad_gain_one: float32 [768], P('col')
- grad_shift_one: float32 [768], P('col')
- grad_w_qkv: float32 [768, 2304], P('col')
- grad_bias_q: float32 [768], P('col')
- grad_bias_v: float32 [768], P('col')
- grad_w_out: float32 [768, 768], P('col')
- grad_bias_out: float32 [768], P('col')
- grad_gain_two: float32 [768], P('col')
- grad_shift_two: float32 [768], P('col')
- grad_w_up: float32 [768, 3072], P('col')
- grad_bias_up: float32 [3072], P('col')
- grad_w_down: float32 [3072, 768], P('col')
- grad_bias_down: float32 [768], P('col')
Inputs may be any that keep to these rules, and one draw needn't show every extreme that they name: In each row the 4 lengths sum to 1024, and the longest is exactly 960.
All inputs are finite; a program needn't handle non-finite values.
Results may differ from a plain program's by a relative error of at most 0.022.
Values may be sent and summed in bfloat16 or wider, within the bound.
A program may use at most 256 MiB of HBM per device.

v0:
```python
import jax
import jax.numpy as jnp
from jax import lax
from jax.sharding import PartitionSpec as P

H = 12
HEAD = 64


epsilon = 1e-05


def layer_norm(values, scales, offset):
    average = jnp.mean(values, axis=-1, keepdims=True)
    centered = values - average
    spread = jnp.mean(centered * centered, axis=-1, keepdims=True)
    return centered * lax.rsqrt(spread + epsilon) * scales + offset


def documents(places, row_lengths):
    finish = jnp.cumsum(row_lengths)
    begins = finish - row_lengths
    inside = (places[:, None] >= begins[None, :]) & (places[:, None] < finish[None, :])
    numbers = jnp.arange(row_lengths.shape[0], dtype=jnp.int32)
    doc_index = jnp.sum(jnp.where(inside, numbers[None, :], 0), axis=1)
    first_place = jnp.sum(jnp.where(inside, begins[None, :], 0), axis=1)
    return (doc_index, first_place == places)


def per_device(
    inputs,
    gain_one,
    shift_one,
    w_qkv,
    bias_q,
    bias_v,
    w_out,
    bias_out,
    gain_two,
    shift_two,
    w_up,
    bias_up,
    w_down,
    bias_down,
    lengths,
    cotangent,
):
    col_count = lax.axis_size("col")
    col_place = lax.axis_index("col")
    tok_rows = inputs.shape[0]
    model_width = inputs.shape[1]
    row_len = tok_rows * col_count
    block_rows = min(512, row_len)
    block_count = row_len // block_rows
    places = jnp.arange(row_len, dtype=jnp.int32)
    doc_index, first_flag = documents(places, lengths[0])
    own_first = col_place * tok_rows
    key_places = own_first + jnp.arange(tok_rows, dtype=jnp.int32)
    key_doc = lax.dynamic_slice_in_dim(doc_index, own_first, tok_rows, 0)
    key_first = lax.dynamic_slice_in_dim(first_flag, own_first, tok_rows, 0)
    floated = inputs.astype(jnp.float32)
    norm_first, first_back = jax.vjp(layer_norm, floated, gain_one, shift_one)
    normed_one = norm_first.astype(jnp.bfloat16)
    joined = jnp.dot(normed_one, w_qkv, preferred_element_type=jnp.float32)
    queries = (joined[:, :model_width] + bias_q).astype(jnp.bfloat16)
    key_rows = joined[:, model_width : 2 * model_width].astype(jnp.bfloat16)
    value_rows = (joined[:, 2 * model_width :] + bias_v).astype(jnp.bfloat16)
    key_heads = key_rows.reshape(tok_rows, H, HEAD)
    value_heads = value_rows.reshape(tok_rows, H, HEAD)
    all_queries = lax.all_gather(queries, "col", axis=0, tiled=True)

    def block_terms(source, block_index, carried):
        first_row = block_index * block_rows
        q_block = lax.dynamic_slice_in_dim(source, first_row, block_rows, 0).reshape(
            block_rows, H, HEAD
        )
        q_places = first_row + jnp.arange(block_rows, dtype=jnp.int32)
        q_doc = lax.dynamic_slice_in_dim(doc_index, first_row, block_rows, 0)
        scores = (
            jnp.einsum("khd,qhd->hkq", key_heads, q_block, preferred_element_type=jnp.float32)
            * 0.125
        )
        allowed = (key_places[:, None] <= q_places[None, :]) & (key_doc[:, None] == q_doc[None, :])
        chosen = (
            allowed
            & (key_places[:, None] < q_places[None, :])
            & jnp.logical_not(key_first)[:, None]
        )
        picked = jnp.where(chosen, jax.nn.softplus(scores[0]), 0.0) / row_len
        forgot = carried[:, None] + jnp.cumsum(picked, axis=1) - picked
        logits = jnp.where(allowed[None], scores - forgot[None], -jnp.inf)
        return (q_block, scores, chosen, picked, logits)

    def forward_block(carried, block_index):
        q_block, scores, chosen, picked, logits = block_terms(all_queries, block_index, carried)
        row_top = jnp.max(logits, axis=1)
        safe_top = jnp.where(row_top > -jnp.inf, row_top, 0.0)
        raised = jnp.exp(logits - safe_top[:, None, :])
        totals = jnp.sum(raised, axis=1)
        numerator = jnp.einsum(
            "hkq,khd->qhd",
            raised.astype(jnp.bfloat16),
            value_heads,
            preferred_element_type=jnp.float32,
        )
        return (
            carried + jnp.sum(picked, axis=1),
            (carried, row_top.T, totals.T, numerator.reshape(block_rows, model_width)),
        )

    indices = jnp.arange(block_count, dtype=jnp.int32)
    unused, (block_starts, row_tops, row_totals, numerators) = lax.scan(
        forward_block, jnp.zeros((tok_rows,), jnp.float32), indices
    )
    row_tops = row_tops.reshape(row_len, H)
    row_totals = row_totals.reshape(row_len, H)
    numerators = numerators.reshape(row_len, model_width)
    got_top, got_total, got_numer = (
        lax.all_to_all(
            row_tops[None].astype(jnp.bfloat16), "col", split_axis=1, concat_axis=0, tiled=True
        ).astype(jnp.float32),
        lax.all_to_all(
            row_totals[None].astype(jnp.bfloat16), "col", split_axis=1, concat_axis=0, tiled=True
        ).astype(jnp.float32),
        lax.all_to_all(
            numerators[None].astype(jnp.bfloat16), "col", split_axis=1, concat_axis=0, tiled=True
        ).astype(jnp.float32),
    )
    row_best = jnp.max(got_top, axis=0)
    factor = jnp.exp(got_top - row_best[None])
    totals_own = jnp.sum(factor * got_total, axis=0)
    numer_own = jnp.sum(got_numer.reshape(col_count, tok_rows, H, HEAD) * factor[..., None], axis=0)
    attended = (numer_own / totals_own[..., None]).reshape(tok_rows, model_width)
    row_lse = row_best + jnp.log(totals_own)
    attended_low = attended.astype(jnp.bfloat16)
    middle = floated + jnp.dot(attended_low, w_out, preferred_element_type=jnp.float32) + bias_out
    norm_second, second_back = jax.vjp(layer_norm, middle, gain_two, shift_two)
    normed_two = norm_second.astype(jnp.bfloat16)
    hidden = jnp.dot(normed_two, w_up, preferred_element_type=jnp.float32) + bias_up
    active_full, gelu_back = jax.vjp(jax.nn.gelu, hidden)
    active = active_full.astype(jnp.bfloat16)
    layer_out = (
        middle + jnp.dot(active, w_down, preferred_element_type=jnp.float32) + bias_down
    ).astype(jnp.bfloat16)
    d_output = cotangent.astype(jnp.float32)
    grad_w_down = jnp.einsum("tf,td->fd", active, cotangent, preferred_element_type=jnp.float32)
    grad_bias_down = jnp.sum(d_output, axis=0)
    d_active = jnp.einsum("td,fd->tf", cotangent, w_down, preferred_element_type=jnp.float32)
    d_hidden = gelu_back(d_active)[0].astype(jnp.bfloat16)
    grad_w_up = jnp.einsum("td,tf->df", normed_two, d_hidden, preferred_element_type=jnp.float32)
    grad_bias_up = jnp.sum(d_hidden.astype(jnp.float32), axis=0)
    d_normed_two = jnp.einsum("tf,df->td", d_hidden, w_up, preferred_element_type=jnp.float32)
    d_middle_norm, grad_gain_two, grad_shift_two = second_back(d_normed_two)
    d_middle = d_output + d_middle_norm
    d_branch = d_middle.astype(jnp.bfloat16)
    grad_w_out = jnp.einsum("td,te->de", attended_low, d_branch, preferred_element_type=jnp.float32)
    grad_bias_out = jnp.sum(d_middle, axis=0)
    d_attended = jnp.einsum(
        "te,de->td", d_branch, w_out, preferred_element_type=jnp.float32
    ).astype(jnp.bfloat16)
    row_delta = jnp.sum(
        (d_attended.astype(jnp.float32) * attended).reshape(tok_rows, H, HEAD), axis=2
    )
    back_queries, gathered_grad = (
        lax.all_gather(queries, "col", axis=0, tiled=True),
        lax.all_gather(d_attended, "col", axis=0, tiled=True),
    )
    all_lse, all_delta = (
        lax.all_gather(row_lse, "col", axis=0, tiled=True),
        lax.all_gather(row_delta, "col", axis=0, tiled=True),
    )

    def backward_block(carried_state, inputs_block):
        later_sum, key_grad, value_grad = carried_state
        block_index, carried = inputs_block
        q_block, scores, chosen, picked, logits = block_terms(back_queries, block_index, carried)
        first_row = block_index * block_rows
        grad_block = lax.dynamic_slice_in_dim(gathered_grad, first_row, block_rows, 0).reshape(
            block_rows, H, HEAD
        )
        lse_block = lax.dynamic_slice_in_dim(all_lse, first_row, block_rows, 0)
        delta_block = lax.dynamic_slice_in_dim(all_delta, first_row, block_rows, 0)
        weights = jnp.exp(logits - lse_block.T[:, None, :])
        value_grad = value_grad + jnp.einsum(
            "hkq,qhd->khd",
            weights.astype(jnp.bfloat16),
            grad_block,
            preferred_element_type=jnp.float32,
        )
        d_weights = jnp.einsum(
            "khd,qhd->hkq", value_heads, grad_block, preferred_element_type=jnp.float32
        )
        d_logits = weights * (d_weights - delta_block.T[:, None, :])
        d_forgot = -jnp.sum(d_logits, axis=0)
        block_sum = jnp.sum(d_forgot, axis=1)
        d_picked = later_sum[:, None] + block_sum[:, None] - jnp.cumsum(d_forgot, axis=1)
        d_select = jnp.where(chosen, jax.nn.sigmoid(scores[0]) * d_picked / row_len, 0.0)
        d_scores = d_logits.at[0].add(d_select).astype(jnp.bfloat16)
        key_grad = (
            key_grad
            + jnp.einsum("hkq,qhd->khd", d_scores, q_block, preferred_element_type=jnp.float32)
            * 0.125
        )
        query_grad = (
            jnp.einsum("hkq,khd->qhd", d_scores, key_heads, preferred_element_type=jnp.float32)
            * 0.125
        )
        return (
            (later_sum + block_sum, key_grad, value_grad),
            query_grad.reshape(block_rows, model_width),
        )

    zero_heads = jnp.zeros((tok_rows, H, HEAD), jnp.float32)
    initial = (jnp.zeros((tok_rows,), jnp.float32), zero_heads, zero_heads)
    (unused_sum, key_grad, value_grad), query_parts = lax.scan(
        backward_block, initial, (indices, block_starts), reverse=True
    )
    query_parts = query_parts.reshape(row_len, model_width)
    d_queries = lax.psum_scatter(query_parts, "col", scatter_dimension=0, tiled=True).astype(
        jnp.bfloat16
    )
    d_keys = key_grad.reshape(tok_rows, model_width).astype(jnp.bfloat16)
    d_values = value_grad.reshape(tok_rows, model_width).astype(jnp.bfloat16)
    d_joined = jnp.concatenate([d_queries, d_keys, d_values], axis=1)
    grad_w_qkv = jnp.einsum("td,te->de", normed_one, d_joined, preferred_element_type=jnp.float32)
    grad_bias_q = jnp.sum(d_queries.astype(jnp.float32), axis=0)
    grad_bias_v = jnp.sum(d_values.astype(jnp.float32), axis=0)
    d_normed_one = jnp.einsum("te,de->td", d_joined, w_qkv, preferred_element_type=jnp.float32)
    d_input_norm, grad_gain_one, grad_shift_one = first_back(d_normed_one)
    grad_inputs = (d_middle + d_input_norm).astype(jnp.bfloat16)
    (
        shard_gain_one,
        shard_shift_one,
        shard_w_qkv,
        shard_bias_q,
        shard_bias_v,
        shard_w_out,
        shard_bias_out,
        shard_gain_two,
        shard_shift_two,
        shard_w_up,
        shard_bias_up,
        shard_w_down,
        shard_bias_down,
    ) = (
        lax.psum_scatter(grad_gain_one, "col", scatter_dimension=0, tiled=True),
        lax.psum_scatter(grad_shift_one, "col", scatter_dimension=0, tiled=True),
        lax.psum_scatter(grad_w_qkv, "col", scatter_dimension=0, tiled=True),
        lax.psum_scatter(grad_bias_q, "col", scatter_dimension=0, tiled=True),
        lax.psum_scatter(grad_bias_v, "col", scatter_dimension=0, tiled=True),
        lax.psum_scatter(grad_w_out, "col", scatter_dimension=0, tiled=True),
        lax.psum_scatter(grad_bias_out, "col", scatter_dimension=0, tiled=True),
        lax.psum_scatter(grad_gain_two, "col", scatter_dimension=0, tiled=True),
        lax.psum_scatter(grad_shift_two, "col", scatter_dimension=0, tiled=True),
        lax.psum_scatter(grad_w_up, "col", scatter_dimension=0, tiled=True),
        lax.psum_scatter(grad_bias_up, "col", scatter_dimension=0, tiled=True),
        lax.psum_scatter(grad_w_down, "col", scatter_dimension=0, tiled=True),
        lax.psum_scatter(grad_bias_down, "col", scatter_dimension=0, tiled=True),
    )
    summed = (
        lax.psum(shard_gain_one.astype(jnp.bfloat16), "dp").astype(jnp.float32),
        lax.psum(shard_shift_one.astype(jnp.bfloat16), "dp").astype(jnp.float32),
        lax.psum(shard_w_qkv.astype(jnp.bfloat16), "dp").astype(jnp.float32),
        lax.psum(shard_bias_q.astype(jnp.bfloat16), "dp").astype(jnp.float32),
        lax.psum(shard_bias_v.astype(jnp.bfloat16), "dp").astype(jnp.float32),
        lax.psum(shard_w_out.astype(jnp.bfloat16), "dp").astype(jnp.float32),
        lax.psum(shard_bias_out.astype(jnp.bfloat16), "dp").astype(jnp.float32),
        lax.psum(shard_gain_two.astype(jnp.bfloat16), "dp").astype(jnp.float32),
        lax.psum(shard_shift_two.astype(jnp.bfloat16), "dp").astype(jnp.float32),
        lax.psum(shard_w_up.astype(jnp.bfloat16), "dp").astype(jnp.float32),
        lax.psum(shard_bias_up.astype(jnp.bfloat16), "dp").astype(jnp.float32),
        lax.psum(shard_w_down.astype(jnp.bfloat16), "dp").astype(jnp.float32),
        lax.psum(shard_bias_down.astype(jnp.bfloat16), "dp").astype(jnp.float32),
    )
    return (
        layer_out,
        grad_inputs,
        summed[0],
        summed[1],
        summed[2],
        summed[3],
        summed[4],
        summed[5],
        summed[6],
        summed[7],
        summed[8],
        summed[9],
        summed[10],
        summed[11],
        summed[12],
    )


def solution(mesh):
    return jax.shard_map(
        per_device,
        mesh=mesh,
        in_specs=(
            P(("dp", "col"), None),
            P(),
            P(),
            P(),
            P(),
            P(),
            P(),
            P(),
            P(),
            P(),
            P(),
            P(),
            P(),
            P(),
            P("dp", None),
            P(("dp", "col"), None),
        ),
        out_specs=(
            P(("dp", "col"), None),
            P(("dp", "col"), None),
            P("col"),
            P("col"),
            P("col", None),
            P("col"),
            P("col"),
            P("col", None),
            P("col"),
            P("col"),
            P("col"),
            P("col", None),
            P("col"),
            P("col", None),
            P("col"),
        ),
        check_vma=False,
    )
```

profile of v0, /device:TPU:0, one launch (start us, length us, event | category | flops | bytes accessed | tf_op | source)
XLA Modules:
  0.0 759.4 jit_solution(689924855866024201)
XLA Ops:
  21.1 21.1 %all-gather.3.cloned.1.call-done = bf16[1024,768]{1,0:T(8,128)(2,1)} async-done(((bf16[128,768]{1,0:T(8,128)(2,1)}), bf16[1024,768]{1,0:T(8,128)(2,1)}) %all-gather.3.cloned.1.call-update) | async-done | bytes 1572880 | tf_op jit(solution)/shard_map/all_gather | solution.py:70
  44.8 65.4 %while.43 = (s32[]{:T(128)}, f32[128]{0:T(128)}, f32[2,128]{1,0:T(2,128)}, bf16[2,512,12]{1,2,0:T(8,128)(2,1)}, bf16[2,512,12]{1,2,0:T(8,128)(2,1)}, /*index=5*/...) while((s32[]{:T(128)}, f32[128]{0:T(128)}, ...), condition=%wide.region_11.12_spmd.clone, body=%wide.region_5.11_spmd.clone.sunk | while | flops 222302336 | bytes 51834048 | solution.py:112
  135.4 4.6 all-to-all-start.2
  140.0 5.5 copy.286
  145.5 12.4 %reduce.10 = bf16[1024,768]{1,0:T(8,128)(2,1)} reduce(bf16[1024,1,768]{2,1,0:T(2,128)(2,1)} %bitcast.288, bf16[]{:T(256)} %broadcast.1093), dimensions={1}, to_apply=%bitcast.160.reduce_sub_computation | reduce | bytes 3145730
  161.6 4.5 all-to-all-start
  166.1 5.3 fusion.156
  187.1 6.3 reshape.1077
  209.4 6.6 convert_reduce_fusion
  222.0 9.1 %all_gather.14 = f32[1024,12]{0,1:T(8,128)} all-gather(f32[128,12]{0,1:T(8,128)S(1)} %log_add_fusion), channel_id=1, replica_groups=mesh['dp'=4,'col'=8] {'col'}, dimensions={0}, use_global_device_ids=true | all-gather | bytes 55296 | tf_op jit(solution)/shard_map/all_gather | solution.py:169
  234.0 10.7 %all_gather.16 = f32[1024,12]{0,1:T(8,128)} all-gather(f32[128,12]{0,1:T(8,128)S(1)} %reduce_sum.294), channel_id=1, replica_groups=mesh['dp'=4,'col'=8] {'col'}, dimensions={0}, use_global_device_ids=true | all-gather | bytes 55296 | tf_op jit(solution)/shard_map/all_gather | solution.py:170
  248.3 95.4 %while.44 = (s32[]{:T(128)}, f32[128]{0:T(128)}, f32[128,12,64]{0,2,1:T(8,128)}, f32[128,12,64]{0,2,1:T(8,128)}, f32[2,512,768]{2,1,0:T(8,128)}, /*index=5*/s32[...) while((s32[]{:T(128)}, f32[128]{0:T(128)}, ...), condition=%wide.region_27.28_spmd.clone, body=%wide.region_20.27_spmd.clone.sunk | while | flops 535074944 | bytes 99309384 | solution.py:215
  347.5 6.9 fusion.149
  355.2 6.5 fusion.147
  368.8 21.4 %reduce-scatter.6.cloned.1.call-done = f32[128,768]{1,0:T(8,128)} async-done(((f32[1024,768]{1,0:T(8,128)}), f32[128,768]{1,0:T(8,128)}) %reduce-scatter.6.cloned.1.call-update) | async-done | bytes 393232 | tf_op jit(solution)/shard_map/reduce_scatter | solution.py:219
  392.4 5.3 fusion.130
  398.0 38.2 %reduce-scatter.10.cloned.1.call-done = f32[96,768]{1,0:T(8,128)} async-done(((f32[768,768]{1,0:T(8,128)}), f32[96,768]{1,0:T(8,128)}) %reduce-scatter.10.cloned.1.call-update) | async-done | bytes 294928 | tf_op jit(solution)/shard_map/reduce_scatter | solution.py:251
  437.9 78.2 %reduce-scatter.14.cloned.1.call-done = f32[384,768]{1,0:T(8,128)} async-done(((f32[3072,768]{1,0:T(8,128)}), f32[384,768]{1,0:T(8,128)}) %reduce-scatter.14.cloned.1.call-update) | async-done | bytes 1179664 | tf_op jit(solution)/shard_map/reduce_scatter | solution.py:257
  518.2 77.7 %reduce-scatter.12.cloned.1.call-done = f32[96,3072]{1,0:T(8,128)} async-done(((f32[768,3072]{1,0:T(8,128)}), f32[96,3072]{1,0:T(8,128)}) %reduce-scatter.12.cloned.1.call-update) | async-done | bytes 1179664 | tf_op jit(solution)/shard_map/reduce_scatter | solution.py:255
  598.1 66.9 %reduce-scatter.8.cloned.1.call-done = f32[96,2304]{1,0:T(8,128)} async-done(((f32[768,2304]{1,0:T(8,128)}), f32[96,2304]{1,0:T(8,128)}) %reduce-scatter.8.cloned.1.call-update) | async-done | bytes 884752 | tf_op jit(solution)/shard_map/reduce_scatter | solution.py:248
  668.9 4.6 fusion.116
  680.0 26.2 %all-reduce.9 = (bf16[768]{0:T(1024)(128)(2,1)}, bf16[768]{0:T(1024)(128)(2,1)}, bf16[768]{0:T(1024)(128)(2,1)}, bf16[768]{0:T(1024)(128)(2,1)}, bf16[768]{0:T(1...) all-reduce(f32[768]{0:T(1024)} %get-tuple-element.828, ...), channel_id=3, replica_groups=mesh['dp'=4,'col'=8] {'col'}, use_global_device_ids=true, to_apply=%region_32.33.clone | all-reduce | flops 9216 | bytes 55296
  714.5 13.2 %all-reduce.10 = (bf16[96]{0:T(256)(128)(2,1)}, bf16[96]{0:T(256)(128)(2,1)}, bf16[96]{0:T(256)(128)(2,1)}, bf16[96]{0:T(256)(128)(2,1)}, bf16[96]{0:T(256)(128)...) all-reduce(bf16[96]{0:T(256)(128)(2,1)S(1)} %dynamic-slice.44, ...), channel_id=1, replica_groups=mesh['dp'=4,'col'=8] {'dp'}, use_global_device_ids=true, to_apply=%region_33.34 | all-reduce | flops 1152 | bytes 4608 | tf_op jit(solution)/shard_map/psum | solution.py:261
  737.6 8.6 %all-reduce.14.cloned.1.call-done = (bf16[96,2304]{1,0:T(8,128)(2,1)}, bf16[96,768]{1,0:T(8,128)(2,1)}, bf16[96,3072]{1,0:T(8,128)(2,1)}, bf16[384,768]{1,0:T(8,128)(2,1)}) async-done(((bf16[96,2304]{1,0:T(8,128)(2,1)}, bf16[96,768]{1,0:T(8,128)(2,1)}, bf16[96,3072]{1,0:T(8,128)(2,1)}, bf16[384,768]{1,0:T(8,128)(2,1)}), (bf16[96,2304]{1,0:T(8,128)(2,1)}, bf16[96,768]{1,0:T(8,128)(2,1)}, ...) | async-done | bytes 1769488 | tf_op jit(solution)/shard_map/psum | solution.py:263
  (519 shorter events, 299.8 us)
Async XLA Ops:
  7.2 35.0 %all-gather.3.cloned.1.call-start = ((), (), s32[]{:S(2)}) async-start(), calls=%async_computation.8 | async-start | bytes 1769472 | tf_op jit(solution)/shard_map/all_gather | solution.py:70
  44.8 18.9 %copy-start.33 = (s32[128]{0:T(128)}, s32[128]{0:T(128)S(1)}, u32[]{:S(2)}) copy-start(s32[128]{0:T(128)S(1)} %get-tuple-element.1193) | copy-start | bytes 1540 | tf_op jit(solution)/shard_map/while
  54.7 9.0 %copy-start.41 = (pred[128,1]{0,1:T(4,128)(4,1)S(1)}, pred[128,1]{0,1:T(4,128)(4,1)}, u32[]{:S(2)}) copy-start(pred[128,1]{0,1:T(4,128)(4,1)} %get-tuple-element.1195) | copy-start | bytes 388 | tf_op jit(solution)/shard_map/while
  77.5 8.0 %copy-start.38 = (s32[1024]{0:T(1024)}, s32[1024]{0:T(1024)S(1)}, u32[]{:S(2)}) copy-start(s32[1024]{0:T(1024)S(1)} %get-tuple-element.1194) | copy-start | bytes 12292 | tf_op jit(solution)/shard_map/while
  77.5 18.9 %copy-start.33 = (s32[128]{0:T(128)}, s32[128]{0:T(128)S(1)}, u32[]{:S(2)}) copy-start(s32[128]{0:T(128)S(1)} %get-tuple-element.1193) | copy-start | bytes 1540 | tf_op jit(solution)/shard_map/while
  87.4 9.0 %copy-start.41 = (pred[128,1]{0,1:T(4,128)(4,1)S(1)}, pred[128,1]{0,1:T(4,128)(4,1)}, u32[]{:S(2)}) copy-start(pred[128,1]{0,1:T(4,128)(4,1)} %get-tuple-element.1195) | copy-start | bytes 388 | tf_op jit(solution)/shard_map/while
  121.1 14.3 %all-to-all-start.1 = ((bf16[8,2,768]{2,1,0:T(2,128)(2,1)}), bf16[8,2,768]{2,1,0:T(2,128)(2,1)}, u32[]{:S(2)}, u32[]{:S(2)}) async-start(bf16[8,2,768]{2,1,0:T(2,128)(2,1)} %reshape.1078), calls=%async_computation.1 | async-start | bytes 49152 | tf_op jit(solution)/shard_map/all_to_all | solution.py:119
  135.4 26.2 %all-to-all-start.2 = ((bf16[8,2,768]{2,1,0:T(2,128)(2,1)}), bf16[8,2,768]{2,1,0:T(2,128)(2,1)}, u32[]{:S(2)}, u32[]{:S(2)}) async-start(bf16[8,2,768]{2,1,0:T(2,128)(2,1)} %reshape.1080), calls=%async_computation.2 | async-start | bytes 49152 | tf_op jit(solution)/shard_map/all_to_all | solution.py:122
  161.6 25.5 %all-to-all-start = ((bf16[8,2,49152]{2,1,0:T(2,128)(2,1)}), bf16[8,2,49152]{2,1,0:T(2,128)(2,1)}, u32[]{:S(2)}, u32[]{:S(2)}) async-start(bf16[8,2,49152]{2,1,0:T(2,128)(2,1)} %reshape.1076), calls=%async_computation | async-start | bytes 3145728 | tf_op jit(solution)/shard_map/all_to_all | solution.py:125
  166.1 80.4 %all-gather.5.cloned.1.call-start = ((), (), s32[]{:S(2)}) async-start(), calls=%async_computation.9 | async-start | bytes 1769472 | tf_op jit(solution)/shard_map/all_gather | solution.py:166
  183.7 20.7 %copy-start.52 = (f32[128,12]{0,1:T(8,128)}, f32[128,12]{0,1:T(8,128)S(1)}, u32[]{:S(2)}) copy-start(f32[128,12]{0,1:T(8,128)S(1)} %get-tuple-element.937) | copy-start | bytes 18436
  207.1 8.9 %slice-start = ((s8[4718592]{0:T(1024)(128)(4,1)}), s8[4194304]{0:T(1024)(128)(4,1)S(1)}, s32[]{:S(2)}) async-start(s8[4718592]{0:T(1024)(128)(4,1)} %bitcast.297), calls=%async_computation.16 | async-start | bytes 8388608
  209.1 9.2 %copy-start.16 = (f32[128,768]{1,0:T(8,128)}, f32[128,768]{1,0:T(8,128)S(1)}, u32[]{:S(2)}) copy-start(f32[128,768]{1,0:T(8,128)S(1)} %get-tuple-element.940) | copy-start | bytes 1179652
  209.2 9.2 %copy-start.63 = (f32[128]{0:T(128)}, f32[128]{0:T(128)S(1)}, u32[]{:S(2)}) copy-start(f32[128]{0:T(128)S(1)} %broadcast_multiply_fusion) | copy-start | bytes 1540
  209.4 9.0 %copy-start.69 = (f32[128]{0:T(128)}, f32[128]{0:T(128)S(1)}, u32[]{:S(2)}) copy-start(f32[128]{0:T(128)S(1)} %fusion.140) | copy-start | bytes 1540
  221.2 169.0 %reduce-scatter.6.cloned.1.call-start = ((), (), s32[]{:S(2)}) async-start(), calls=%async_computation.10 | async-start | bytes 3538944 | tf_op jit(solution)/shard_map/reduce_scatter | solution.py:219
  343.7 92.5 %reduce-scatter.10.cloned.1.call-start = ((), (), s32[]{:S(2)}) async-start(), calls=%async_computation.12 | async-start | bytes 2654208 | tf_op jit(solution)/shard_map/reduce_scatter | solution.py:251
  347.5 168.6 %reduce-scatter.14.cloned.1.call-start = ((), (), s32[]{:S(2)}) async-start(), calls=%async_computation.14 | async-start | bytes 10616832 | tf_op jit(solution)/shard_map/reduce_scatter | solution.py:257
  354.5 241.5 %reduce-scatter.12.cloned.1.call-start = ((), (), s32[]{:S(2)}) async-start(), calls=%async_computation.13 | async-start | bytes 10616832 | tf_op jit(solution)/shard_map/reduce_scatter | solution.py:255
  361.7 30.7 %copy-start.47 = (f32[768]{0:T(1024)S(1)}, f32[768]{0:T(1024)}, u32[]{:S(2)}) copy-start(f32[768]{0:T(1024)} %param.23) | copy-start | bytes 9220
  361.7 30.7 %copy-start.51 = (f32[768]{0:T(1024)S(1)}, f32[768]{0:T(1024)}, u32[]{:S(2)}) copy-start(f32[768]{0:T(1024)} %param.24) | copy-start | bytes 9220
  361.7 303.3 %reduce-scatter.8.cloned.1.call-start = ((), (), s32[]{:S(2)}) async-start(), calls=%async_computation.11 | async-start | bytes 7962624 | tf_op jit(solution)/shard_map/reduce_scatter | solution.py:248
  397.7 348.4 %all-reduce.14.cloned.1.call-start = ((), (), s32[]{:S(2)}) async-start(), calls=%async_computation.15 | async-start | bytes 3538944 | tf_op jit(solution)/shard_map/psum | solution.py:263
  598.1 68.9 %copy-start.79 = (u32[32]{0:T(128)S(1)}, u32[32]{0:T(128)}, u32[]{:S(2)}) copy-start(u32[32]{0:T(128)} %constant.248) | copy-start | bytes 388
  (114 other events, 281.8 us)
Sparse Core Ops, SparseCore 0:
  13.8 28.3 all-gather.2
  221.3 25.0 all-gather.4
  343.9 46.2 reduce-scatter.5
  393.7 42.4 reduce-scatter.9
  439.6 76.4 reduce-scatter.13
  519.4 76.4 reduce-scatter.11
  599.5 65.5 reduce-scatter.7
  669.0 77.1 all-reduce.13
where the time goes:
time: 772 us; the launch traced here: 759 us
  waiting for transfers between devices  317 us (41%)
  local copies, waits for them, and re-layouts  154 us (20%)
  other arithmetic  116 us (15%)
  matrix products  79.5 us (10%)
  blocking collectives  59.1 us (8%)
  between operations  16.4 us (2%)
  starting transfers between devices  13.6 us (2%)
    reduce_scatter x1, waiting for transfers between devices, per_device(): lax.psum_scatter(grad_w_down, 'col', scatter_dimension=0, tiled=True)  78.2 us
    reduce_scatter x1, waiting for transfers between devices, per_device(): lax.psum_scatter(grad_w_up, 'col', scatter_dimension=0, tiled=True)  77.7 us
    reduce_scatter x1, waiting for transfers between devices, per_device(): lax.psum_scatter(grad_w_qkv, 'col', scatter_dimension=0, tiled=True)  66.9 us
    unnamed x110, local copies, waits for them, and re-layouts  38.8 us
    reduce_scatter x1, waiting for transfers between devices, per_device(): lax.psum_scatter(grad_w_out, 'col', scatter_dimension=0, tiled=True)  38.2 us
    unnamed x1, blocking collectives  26.2 us
    dynamic_update_slice x14, local copies, waits for them, and re-layouts, per_device(): lax.scan(forward_block, jnp.zeros((tok_rows,), jnp.float32), indices)  25.1 us
    reduce_scatter x1, waiting for transfers between devices, per_device(): lax.psum_scatter(query_parts, 'col', scatter_dimension=0, tiled=True)  21.4 us
  transfers between devices with their start and end apart: 11, of which 9 were waited for; matrix products, arithmetic and copies ran while one was open for 17% of the time, Pallas kernels for 0%

commit v1 on v0

--- a/solution.py
+++ b/solution.py
@@ -1,6 +1,11 @@
+import functools
+import types
+
 import jax
 import jax.numpy as jnp
 from jax import lax
+from jax.experimental import pallas as pl
+from jax.experimental.pallas import tpu as pltpu
 from jax.sharding import PartitionSpec as P
 
 H = 12
@@ -27,7 +32,7 @@
     return (doc_index, first_place == places)
 
 
-def per_device(
+def general_device(
     inputs,
     gain_one,
     shift_one,
@@ -291,6 +296,839 @@
     )
 
 
+MESH = pl.DeviceIdType.MESH
+LOW = jnp.bfloat16
+WIDE = jnp.float32
+FAR = 1e30
+ROW_UNITS = 12
+
+
+def dot(a, b):
+    return jnp.dot(a, b, preferred_element_type=WIDE)
+
+
+def dot_rows(a, b):
+    return lax.dot_general(a, b, (((1,), (1,)), ((), ())), preferred_element_type=WIDE)
+
+
+def split_low(values):
+    high = values.astype(LOW)
+    return high, (values - high.astype(WIDE)).astype(LOW)
+
+
+def norm_parts(values):
+    average = jnp.mean(values, axis=-1, keepdims=True)
+    centered = values - average
+    spread = jnp.mean(centered * centered, axis=-1, keepdims=True)
+    scale = lax.rsqrt(spread + epsilon)
+    return centered * scale, scale
+
+
+def norm_back(grad, unit, scale, gain):
+    scaled = grad * gain
+    first = jnp.mean(scaled, axis=-1, keepdims=True)
+    second = jnp.mean(scaled * unit, axis=-1, keepdims=True)
+    return scale * (scaled - first - unit * second)
+
+
+SCRATCH = dict(
+    wqkv=((768, 2304), LOW),
+    wout=((768, 768), LOW),
+    wup=((768, 3072), LOW),
+    wdown=((32, 96, 768), LOW),
+    kv=((3, 8, 2, 128, 256), LOW),
+    turned=((6, 128, 1024), LOW),
+    probs=((6, 1024, 256), LOW),
+    sums=((8, 8, 128), WIDE),
+    back_sums=((8, 8, 128), WIDE),
+    forgot=((128, 1024), WIDE),
+    forgot_t=((1024, 128), WIDE),
+    sig_t=((1024, 128), WIDE),
+    d_forgot_t=((1024, 128), WIDE),
+    second_head=((1024, 128), LOW),
+    q_low=((128, 768), LOW),
+    q_turned=((768, 128), LOW),
+    n1_t=((8, 96, 128), LOW),
+    n2_t=((8, 96, 128), LOW),
+    att_t=((768, 128), WIDE),
+    att_low_t=((8, 96, 128), LOW),
+    act=((128, 3072), LOW),
+    act_t=((8, 4, 96, 128), LOW),
+    d_act=((128, 3072), WIDE),
+    middle=((128, 768), WIDE),
+    d_mid=((128, 768), WIDE),
+    unit_two=((128, 768), WIDE),
+    d_att=((128, 768), LOW),
+    d_att_t=((768, 128), LOW),
+    dq_t=((768, 128), WIDE),
+    cot2=((256, 768), LOW),
+    dh2=((256, 3072), LOW),
+    db2=((256, 768), LOW),
+    dqkv2=((256, 2304), LOW),
+    lhs_down=((4, 4, 96, 256), LOW),
+    lhs_up=((4, 96, 256), LOW),
+    lhs_out=((4, 96, 256), LOW),
+    lhs_qkv=((4, 96, 256), LOW),
+    give_down=((4, 4, 96, 128), LOW),
+    give_up=((4, 96, 128), LOW),
+    give_out=((4, 96, 128), LOW),
+    give_qkv=((4, 96, 128), LOW),
+    dkv=((3, 2, 2, 4, 128, 256), LOW),
+    dkv_core=((3, 2, 4, 128, 256), LOW),
+    dkv_one=((3, 2, 2, 128, 256), LOW),
+    dkv_two=((3, 2, 128, 256), LOW),
+    part=((4, 4, 96, 768), LOW),
+    got_one=((ROW_UNITS, 2, 2, 96, 384), LOW),
+    got_two=((ROW_UNITS, 2, 96, 384), LOW),
+    mine=((ROW_UNITS, 2, 48, 768), LOW),
+    got_z=((ROW_UNITS, 48, 768), LOW),
+    got_zz=((ROW_UNITS, 48, 768), LOW),
+    total=((ROW_UNITS, 2, 48, 768), LOW),
+    small=((6, 8, 1152), WIDE),
+    small_got=((5, 8, 1152), WIDE),
+)
+
+
+def layer_kernel(
+    lengths_ref,
+    x_ref,
+    cot_ref,
+    gain_one,
+    shift_one,
+    bias_q,
+    bias_v,
+    bias_out,
+    gain_two,
+    shift_two,
+    bias_up,
+    bias_down,
+    w_qkv,
+    w_out,
+    w_up,
+    w_down,
+    out_ref,
+    grad_ref,
+    total_ref,
+    small_ref,
+    wide_ref,
+    *scratch,
+):
+    s = types.SimpleNamespace(**dict(zip(SCRATCH, scratch)))
+    sent, landed, local = scratch[len(SCRATCH) :]
+    me = lax.axis_index("col")
+    dp = lax.axis_index("dp")
+    core = lax.rem(me, 2)
+    x_bit = lax.rem(lax.div(me, 2), 2)
+    y_bit = lax.div(me, 4)
+    z_low = lax.rem(dp, 2)
+    z_high = lax.div(dp, 2)
+
+    def place(r):
+        step = (r & 1) * (1 - 2 * core) + ((r >> 1) & 1) * (2 - 4 * x_bit)
+        return me + step + (r >> 2) * (4 - 8 * y_bit)
+
+    def near(r):
+        return (dp, place(r))
+
+    z_one = (dp + 1 - 2 * z_low, me)
+    z_two = (dp + 2 - 4 * z_high, me)
+    messages = []
+
+    def send(source, target, device):
+        at = len(messages)
+        copy = pltpu.make_async_remote_copy(
+            src_ref=source,
+            dst_ref=target,
+            send_sem=sent.at[at],
+            recv_sem=landed.at[at],
+            device_id=device,
+            device_id_type=MESH,
+        )
+        copy.start()
+        messages.append(copy)
+        return copy
+
+    loads = {}
+    for at, (name, source, target) in enumerate(
+        (
+            ("qkv", w_qkv, s.wqkv),
+            ("down", w_down, s.wdown),
+            ("out", w_out, s.wout),
+            ("up", w_up, s.wup),
+        )
+    ):
+        loads[name] = pltpu.make_async_copy(source, target, local.at[at])
+        loads[name].start()
+
+    barrier = pltpu.get_barrier_semaphore()
+    for device in [near(r) for r in range(1, 8)] + [z_one, z_two]:
+        pl.semaphore_signal(barrier, inc=1, device_id=device, device_id_type=MESH)
+
+    values_one = x_ref[...].astype(WIDE)
+    unit_one, scale_one = norm_parts(values_one)
+    normed_one = (unit_one * gain_one[...] + shift_one[...]).astype(LOW)
+    loads["qkv"].wait()
+    pl.semaphore_wait(barrier, 9)
+    s.cot2[0:128, :] = cot_ref[...]
+    gather = []
+    for g in range(3):
+        at = 256 * g
+        s.kv[g, 0, 0] = dot(normed_one, s.wqkv[:, 768 + at : 1024 + at]).astype(LOW)
+        s.kv[g, 0, 1] = (
+            dot(normed_one, s.wqkv[:, 1536 + at : 1792 + at]) + bias_v[:, at : at + 256]
+        ).astype(LOW)
+        gather.append([send(s.kv.at[g, 0], s.kv.at[g, r], near(r)) for r in (2, 4, 1)])
+    share_cot = send(s.cot2.at[pl.ds(0, 128)], s.cot2.at[pl.ds(128, 128)], near(1))
+    for g in range(3):
+        at = 256 * g
+        q = (dot(normed_one, s.wqkv[:, at : at + 256]) + bias_q[:, at : at + 256]).astype(LOW)
+        q = (q.astype(WIDE) * 0.125).astype(LOW)
+        s.q_low[:, at : at + 256] = q
+        s.q_turned[at : at + 256, :] = q.T
+
+    def share(source, lhs, give):
+        for slot, r in enumerate((0, 2, 6, 4)):
+            ours = place(r)
+            lhs[slot, ..., 0:128] = source[ours]
+            give[slot] = source[ours + 1 - 2 * core]
+        return send(give, lhs.at[..., pl.ds(128, 128)], near(1))
+
+    s.n1_t[...] = normed_one.T.reshape(8, 96, 128)
+    share_one = share(s.n1_t, s.lhs_qkv, s.give_qkv)
+
+    more = [[] for _ in range(3)]
+    diagonal = [[] for _ in range(3)]
+
+    def forward(g):
+        gather[g][0].wait_recv()
+        diagonal[g].append(send(s.kv.at[g, 2, 0], s.kv.at[g, 6, 0], near(4)))
+        more[g].append(send(s.kv.at[g, 2], s.kv.at[g, 3], near(1)))
+        gather[g][1].wait_recv()
+        diagonal[g].append(send(s.kv.at[g, 4, 1], s.kv.at[g, 6, 1], near(2)))
+        more[g].append(send(s.kv.at[g, 4], s.kv.at[g, 5], near(1)))
+        gather[g][2].wait_recv()
+
+    def forward_diagonal(g):
+        diagonal[g][0].wait_recv()
+        more[g].append(send(s.kv.at[g, 6, 0], s.kv.at[g, 7, 0], near(1)))
+        diagonal[g][1].wait_recv()
+        more[g].append(send(s.kv.at[g, 6, 1], s.kv.at[g, 7, 1], near(1)))
+
+    def gathered(g):
+        for copy in more[g]:
+            copy.wait_recv()
+
+    def active_grad(first, last):
+        for j in range(first, last):
+            rows = s.wdown[4 * j : 4 * j + 4].reshape(384, 768)
+            s.d_act[:, 384 * j : 384 * j + 384] = dot_rows(cot_ref[...], rows)
+
+    loads["down"].wait()
+    active_grad(0, 3)
+    forward(0)
+    active_grad(3, 5)
+    forward_diagonal(0)
+    forward(1)
+    active_grad(5, 8)
+    gathered(0)
+
+    row_at = lax.broadcasted_iota(jnp.int32, (128, 128), 0)
+    lane_at = lax.broadcasted_iota(jnp.int32, (128, 128), 1)
+    query_at = row_at + me * 128
+    begin_one = lengths_ref[0, 0]
+    begin_two = begin_one + lengths_ref[0, 1]
+    begin_three = begin_two + lengths_ref[0, 2]
+    begin = jnp.where(query_at >= begin_one, begin_one, 0)
+    begin = jnp.where(query_at >= begin_two, begin_two, begin)
+    begin = jnp.where(query_at >= begin_three, begin_three, begin)
+    earlier = jnp.where(lane_at < row_at, 1.0, 0.0).astype(LOW)
+    first_lanes = jnp.where(lane_at < 64, 1.0, 0.0)
+    head_zero = (s.q_low[:, 0:128].astype(WIDE) * first_lanes).astype(LOW)
+    for r in range(8):
+        scores = dot_rows(head_zero, s.kv[0, r, 0, :, 0:128])
+        key_at = lane_at + place(r) * 128
+        allowed = (key_at <= query_at) & (key_at >= begin)
+        chosen = (key_at < query_at) & (key_at > begin)
+        small_exp = jnp.exp(-jnp.abs(scores))
+        soft = jnp.maximum(scores, 0.0) + jnp.log1p(small_exp)
+        picked = jnp.where(chosen, soft, 0.0) * (1.0 / 1024)
+        high, rest = split_low(picked)
+        s.sums[0, r : r + 1, :] = jnp.sum(picked, axis=0, keepdims=True)
+        within = dot(earlier, high) + dot(earlier, rest)
+        s.forgot[:, 128 * r : 128 * r + 128] = jnp.where(allowed, within, FAR)
+        sigmoid = jnp.where(scores >= 0, 1.0, small_exp) / (1.0 + small_exp)
+        s.sig_t[128 * r : 128 * r + 128, :] = (jnp.where(chosen, sigmoid, 0.0) * (1.0 / 1024)).T
+    sum_copies = [send(s.sums.at[0], s.sums.at[r], near(r)) for r in range(1, 8)]
+    forward_diagonal(1)
+    forward(2)
+    gathered(1)
+    for copy in sum_copies:
+        copy.wait_recv()
+
+    def others(sums, later):
+        rows = [jnp.zeros((1, 128), WIDE) for _ in range(8)]
+        for d in range(1, 8):
+            ahead = place(d) > me if later else place(d) < me
+            weight = jnp.where(ahead, 1.0, 0.0)
+            for r in range(8):
+                rows[r] = rows[r] + weight * sums[d, (r ^ d) : (r ^ d) + 1, :]
+        return rows
+
+    for r, row in enumerate(others(s.sums, False)):
+        at = 128 * r
+        s.forgot_t[at : at + 128, :] = (s.forgot[:, at : at + 128] + row).T
+
+    feature_at = lax.broadcasted_iota(jnp.int32, (128, 256), 0)
+    column_at = lax.broadcasted_iota(jnp.int32, (128, 256), 1)
+    own_head_t = jnp.where((feature_at < 64) == (column_at < 128), 1.0, 0.0).astype(LOW)
+    long_row = lax.broadcasted_iota(jnp.int32, (256, 128), 0)
+    long_lane = lax.broadcasted_iota(jnp.int32, (256, 128), 1)
+    own_head = jnp.where((long_row < 128) == (long_lane < 64), 1.0, 0.0).astype(LOW)
+
+    def both_t(values):
+        return jnp.concatenate([values, values], axis=1) * own_head_t
+
+    def both(values):
+        return jnp.concatenate([values, values], axis=0) * own_head
+
+    def block(pair, part):
+        at = 128 * (pair % 2)
+        return s.kv[pair // 2, :, part, :, at : at + 128].reshape(1024, 128)
+
+    def turn(pair, part):
+        at = 128 * (pair % 2)
+        for r in range(8):
+            s.turned[pair, :, 128 * r : 128 * r + 128] = s.kv[
+                pair // 2, r, part, :, at : at + 128
+            ].T
+
+    def attend(pair):
+        at = 128 * pair
+        turn(pair, 1)
+        scores = dot(block(pair, 0), both_t(s.q_turned[at : at + 128, :]))
+        forgot = s.forgot_t[...]
+        logits = scores - jnp.concatenate([forgot, forgot], axis=1)
+        raised = jnp.exp(logits - jnp.max(logits, axis=0, keepdims=True))
+        probs = (raised * (1.0 / jnp.sum(raised, axis=0, keepdims=True))).astype(LOW)
+        s.probs[pair] = probs
+        mixed = dot(s.turned[pair], probs)
+        s.att_t[at : at + 64, :] = mixed[0:64, 0:128]
+        s.att_t[at + 64 : at + 128, :] = mixed[64:128, 128:256]
+
+    attend(0)
+    attend(1)
+    forward_diagonal(2)
+    attend(2)
+    attend(3)
+    gathered(2)
+    attend(4)
+    attend(5)
+
+    attended_low_t = s.att_t[...].astype(LOW)
+    s.att_low_t[...] = attended_low_t.reshape(8, 96, 128)
+    loads["out"].wait()
+    middle = values_one + dot(attended_low_t.T, s.wout[...]) + bias_out[...]
+    s.middle[...] = middle
+    unit_two, scale_two = norm_parts(middle)
+    s.unit_two[...] = unit_two
+    normed_two = (unit_two * gain_two[...] + shift_two[...]).astype(LOW)
+    s.n2_t[...] = normed_two.T.reshape(8, 96, 128)
+    share_two = share(s.n2_t, s.lhs_up, s.give_up)
+    share_att = share(s.att_low_t, s.lhs_out, s.give_out)
+    loads["up"].wait()
+    share_hidden = []
+    for j in range(4):
+        at = 768 * j
+        hidden = dot(normed_two, s.wup[:, at : at + 768]) + bias_up[:, at : at + 768]
+        square = hidden * hidden
+        bend = jnp.tanh(0.7978845608028654 * hidden * (1.0 + 0.044715 * square))
+        half = 0.5 * (1.0 + bend)
+        active = (hidden * half).astype(LOW)
+        slope = half + 0.5 * hidden * (1.0 - bend * bend) * (
+            0.7978845608028654 * (1.0 + 3 * 0.044715 * square)
+        )
+        s.act[:, at : at + 768] = active
+        turned = active.T.reshape(2, 4, 96, 128)
+        s.act_t[2 * j : 2 * j + 2] = turned
+        d_hidden = (s.d_act[:, at : at + 768] * slope).astype(LOW)
+        s.dh2[0:128, at : at + 768] = d_hidden
+        s.small[0, 2 * j : 2 * j + 1, 768:1152] = jnp.sum(
+            d_hidden[:, 0:384].astype(WIDE), axis=0, keepdims=True
+        )
+        s.small[0, 2 * j + 1 : 2 * j + 2, 768:1152] = jnp.sum(
+            d_hidden[:, 384:768].astype(WIDE), axis=0, keepdims=True
+        )
+    share_down = share(s.act_t, s.lhs_down, s.give_down)
+    share_hidden = send(s.dh2.at[pl.ds(0, 128)], s.dh2.at[pl.ds(128, 128)], near(1))
+
+    class Unit:
+        def __init__(self, at, lhs, rhs, grads):
+            self.at, self.lhs, self.rhs, self.grads = at, lhs, rhs, grads
+
+        def make(self):
+            lhs = self.lhs[...].reshape(384, 256)
+            for half in range(2):
+                at = 384 * half
+                grads = dot(lhs, self.rhs[:, at : at + 384]).astype(LOW)
+                self.grads[:, :, at : at + 384] = grads.reshape(4, 96, 384)
+            got = s.got_one.at[self.at]
+            self.one = (
+                send(self.grads.at[pl.ds(1, 2), :, pl.ds(0, 384)], got.at[0], near(2)),
+                send(self.grads.at[pl.ds(2, 2), :, pl.ds(384, 384)], got.at[1], near(4)),
+            )
+
+        def add(self, slot, half, got):
+            at = 384 * half
+            ours = self.grads[slot, :, at : at + 384].astype(WIDE)
+            return ours + got[...].astype(WIDE)
+
+        def pass_on(self):
+            got = s.got_one.at[self.at]
+            two = []
+            for half, slot, index, r in ((0, 3, 1, 4), (1, 1, 0, 2)):
+                at = 384 * half
+                self.one[half].wait_recv()
+                total = self.add(slot, half, got.at[half, index]).astype(LOW)
+                self.grads[slot, :, at : at + 384] = total
+                two.append(
+                    send(
+                        self.grads.at[slot, :, pl.ds(at, 384)],
+                        s.got_two.at[self.at, half],
+                        near(r),
+                    )
+                )
+            self.two = two
+
+        def finish(self):
+            got = s.got_one.at[self.at]
+            for half, index in ((0, 0), (1, 1)):
+                at = 384 * half
+                self.two[half].wait_recv()
+                total = self.add(0, half, got.at[half, index])
+                total = (total + s.got_two[self.at, half].astype(WIDE)).astype(LOW)
+                s.mine[self.at, :, :, at : at + 384] = total.reshape(2, 48, 384)
+            self.z = send(s.mine.at[self.at, 1 - z_low], s.got_z.at[self.at], z_one)
+
+        def z_pair(self):
+            self.z.wait_recv()
+            total = s.mine[self.at, z_low].astype(WIDE) + s.got_z[self.at].astype(WIDE)
+            s.mine[self.at, z_low] = total.astype(LOW)
+            self.z = send(s.mine.at[self.at, z_low], s.got_zz.at[self.at], z_two)
+
+        def z_all(self):
+            self.z.wait_recv()
+            total = s.mine[self.at, z_low].astype(WIDE) + s.got_zz[self.at].astype(WIDE)
+            s.total[self.at, z_low] = total.astype(LOW)
+            self.z = send(s.total.at[self.at, z_low], s.total.at[self.at, z_low], z_one)
+
+        def done(self):
+            self.z.wait_recv()
+            copy = pltpu.make_async_copy(
+                s.total.at[self.at], total_ref.at[self.at], local.at[4 + self.at]
+            )
+            copy.start()
+            writes.append(copy)
+
+    writes = []
+    units = []
+    for j in range(4):
+        units.append(Unit(j, s.lhs_down.at[:, j], s.cot2, s.part.at[j]))
+    spare = [s.wdown.at[pl.ds(4 * j, 4)] for j in range(8)]
+    units.append(Unit(4, s.lhs_out, s.db2, spare[0]))
+    for j in range(4):
+        units.append(Unit(5 + j, s.lhs_up, s.dh2.at[:, pl.ds(768 * j, 768)], spare[1 + j]))
+    for j in range(3):
+        units.append(Unit(9 + j, s.lhs_qkv, s.dqkv2.at[:, pl.ds(768 * j, 768)], spare[5 + j]))
+
+    share_cot.wait_recv()
+    share_down.wait_recv()
+    units[0].make()
+    units[1].make()
+
+    d_output = cot_ref[...].astype(WIDE)
+    parts = []
+    for j in range(3):
+        parts.append(dot_rows(s.dh2[0:128, :], s.wup[256 * j : 256 * j + 256, :]))
+    d_normed = jnp.concatenate(parts, axis=1)
+    unit_two = s.unit_two[...]
+    s.small[0, 5:6, 0:768] = jnp.sum(d_normed * unit_two, axis=0, keepdims=True)
+    s.small[0, 6:7, 0:768] = jnp.sum(d_normed, axis=0, keepdims=True)
+    s.small[0, 7:8, 0:768] = jnp.sum(d_output, axis=0, keepdims=True)
+    d_middle = d_output + norm_back(d_normed, unit_two, scale_two, gain_two[...])
+    s.d_mid[...] = d_middle
+    s.small[0, 4:5, 0:768] = jnp.sum(d_middle, axis=0, keepdims=True)
+    d_branch = d_middle.astype(LOW)
+    s.db2[0:128, :] = d_branch
+    share_branch = send(s.db2.at[pl.ds(0, 128)], s.db2.at[pl.ds(128, 128)], near(1))
+    d_att_t = dot(s.wout[...], d_branch.T).astype(LOW)
+    s.d_att_t[...] = d_att_t
+    s.d_att[...] = d_att_t.T
+
+    mixed = jnp.zeros((128, 768), WIDE)
+    for j in range(4):
+        rows = s.wdown[8 * j : 8 * j + 8].reshape(768, 768)
+        mixed = mixed + dot(s.act[:, 768 * j : 768 * j + 768], rows)
+    out_ref[...] = (s.middle[...] + mixed + bias_down[...]).astype(LOW)
+
+    def logit_grads(pair):
+        at = 128 * pair
+        grad_t = s.d_att_t[at : at + 128, :]
+        products = grad_t.astype(WIDE) * s.att_t[at : at + 128, :]
+        delta = jnp.concatenate(
+            [
+                jnp.sum(products[0:64], axis=0, keepdims=True),
+                jnp.sum(products[64:128], axis=0, keepdims=True),
+            ],
+            axis=1,
+        )
+        d_probs = dot(block(pair, 1), both_t(grad_t))
+        d_logits = s.probs[pair].astype(WIDE) * (d_probs - delta)
+        both_heads = d_logits[:, 0:128] + d_logits[:, 128:256]
+        if pair == 5:
+            s.d_forgot_t[...] = both_heads
+        else:
+            s.d_forgot_t[...] += both_heads
+        return d_logits
+
+    def keep(pair, half, grads):
+        at = 128 * (pair % 2)
+        low = grads.astype(LOW)
+        for r in range(8):
+            slot = (0, 1, 3, 2)[r >> 1]
+            s.dkv[pair // 2, r & 1, half, slot, :, at : at + 128] = low[128 * r : 128 * r + 128]
+
+    def value_grads(pair):
+        at = 128 * pair
+        keep(pair, 1, dot(s.probs[pair], both(s.d_att[:, at : at + 128])))
+
+    def score_grads(pair, d_scores):
+        at = 128 * pair
+        turn(pair, 0)
+        keep(pair, 0, dot(d_scores, both(s.q_low[:, at : at + 128])))
+        grads = dot(s.turned[pair], d_scores)
+        s.dq_t[at : at + 64, :] = grads[0:64, 0:128]
+        s.dq_t[at + 64 : at + 128, :] = grads[64:128, 128:256]
+
+    def attend_back(pair):
+        d_logits = logit_grads(pair)
+        value_grads(pair)
+        score_grads(pair, d_logits.astype(LOW))
+
+    class KeyGroup:
+        def __init__(self, g):
+            self.g = g
+
+        def across(self):
+            self.core = send(s.dkv.at[self.g, 1], s.dkv_core.at[self.g], near(1))
+
+        def make(self):
+            g = self.g
+            self.core.wait_recv()
+            total = s.dkv[g, 0].astype(WIDE) + s.dkv_core[g].astype(WIDE)
+            s.dkv[g, 0] = total.astype(LOW)
+            self.one = (
+                send(s.dkv.at[g, 0, 0, pl.ds(1, 2)], s.dkv_one.at[g, 0], near(2)),
+                send(s.dkv.at[g, 0, 1, pl.ds(2, 2)], s.dkv_one.at[g, 1], near(4)),
+            )
+
+        def pass_on(self):
+            g = self.g
+            two = []
+            for half, slot, index, r in ((0, 3, 1, 4), (1, 1, 0, 2)):
+                self.one[half].wait_recv()
+                total = s.dkv[g, 0, half, slot].astype(WIDE) + s.dkv_one[g, half, index].astype(WIDE)
+                s.dkv[g, 0, half, slot] = total.astype(LOW)
+                two.append(send(s.dkv.at[g, 0, half, slot], s.dkv_two.at[g, half], near(r)))
+            self.two = two
+
+        def finish(self):
+            g = self.g
+            for half, index in ((0, 0), (1, 1)):
+                self.two[half].wait_recv()
+                total = s.dkv[g, 0, half, 0].astype(WIDE) + s.dkv_one[g, half, index].astype(WIDE)
+                total = total + s.dkv_two[g, half].astype(WIDE)
+                at = 768 * (half + 1) + 256 * g
+                s.dqkv2[0:128, at : at + 256] = total.astype(LOW)
+
+    groups = [KeyGroup(g) for g in range(3)]
+    share_two.wait_recv()
+    share_hidden.wait_recv()
+    units[5].make()
+    units[0].pass_on()
+    attend_back(5)
+    units[1].pass_on()
+    units[6].make()
+    attend_back(4)
+    groups[2].across()
+    units[0].finish()
+    attend_back(3)
+    groups[2].make()
+    units[5].pass_on()
+    attend_back(2)
+    groups[1].across()
+    units[1].finish()
+    attend_back(1)
+    groups[1].make()
+    units[6].pass_on()
+    d_logits = logit_grads(0)
+    s.forgot_t[...] = d_logits[:, 0:128]
+    s.second_head[...] = d_logits[:, 128:256].astype(LOW)
+    for r in range(8):
+        turned = s.d_forgot_t[128 * r : 128 * r + 128, :].T
+        s.back_sums[0, r : r + 1, :] = jnp.sum(turned, axis=0, keepdims=True)
+    sum_copies = [send(s.back_sums.at[0], s.back_sums.at[r], near(r)) for r in range(1, 8)]
+    value_grads(0)
+    units[2].make()
+    groups[2].pass_on()
+    units[0].z_pair()
+    units[1].z_pair()
+    for copy in sum_copies:
+        copy.wait_recv()
+    later_rows = others(s.back_sums, True)
+    following = jnp.where(row_at > lane_at, 1.0, 0.0).astype(LOW)
+    selected = []
+    for r in range(8):
+        at = 128 * r
+        high, rest = split_low(s.d_forgot_t[at : at + 128, :])
+        later = jnp.broadcast_to(later_rows[r], (128, 128)).T
+        d_picked = -(dot(high, following) + dot(rest, following) + later)
+        selected.append(s.forgot_t[at : at + 128, :] + s.sig_t[at : at + 128, :] * d_picked)
+    first_head = jnp.concatenate(selected, axis=0).astype(LOW)
+    score_grads(0, jnp.concatenate([first_head, s.second_head[...]], axis=1))
+    groups[0].across()
+    for j in range(6):
+        at = 128 * j
+        d_q = (s.dq_t[at : at + 128, :] * 0.125).astype(LOW)
+        s.dqkv2[0:128, at : at + 128] = d_q.T
+
+    def share_part(j):
+        cols = pl.ds(768 * j, 768)
+        return send(
+            s.dqkv2.at[pl.ds(0, 128), cols], s.dqkv2.at[pl.ds(128, 128), cols], near(1)
+        )
+
+    def input_part(j):
+        cols = slice(768 * j, 768 * j + 768)
+        parts = []
+        for i in range(3):
+            rows = s.wqkv[256 * i : 256 * i + 256, cols]
+            parts.append(dot_rows(s.dqkv2[0:128, cols], rows))
+        return jnp.concatenate(parts, axis=1)
+
+    share_q = share_part(0)
+    units[5].finish()
+    groups[1].pass_on()
+    groups[0].make()
+    groups[2].finish()
+    units[6].finish()
+    units[3].make()
+    units[2].pass_on()
+    units[0].z_all()
+    units[1].z_all()
+    d_normed = input_part(0)
+    groups[0].pass_on()
+    groups[1].finish()
+    share_att.wait_recv()
+    share_branch.wait_recv()
+    share_one.wait_recv()
+    units[4].make()
+    units[3].pass_on()
+    units[2].finish()
+    units[5].z_pair()
+    units[6].z_pair()
+    groups[0].finish()
+    share_k = share_part(1)
+    share_v = share_part(2)
+    share_q.wait_recv()
+    units[9].make()
+    units[4].pass_on()
+    d_normed = d_normed + input_part(1) + input_part(2)
+    share_k.wait_recv()
+    units[10].make()
+    units[9].pass_on()
+    share_v.wait_recv()
+    units[11].make()
+    units[10].pass_on()
+    unit_one, scale_one = norm_parts(x_ref[...].astype(WIDE))
+    s.small[0, 0:1, 0:768] = jnp.sum(d_normed * unit_one, axis=0, keepdims=True)
+    s.small[0, 1:2, 0:768] = jnp.sum(d_normed, axis=0, keepdims=True)
+    s.small[0, 2:3, 0:768] = jnp.sum(
+        s.dqkv2[0:128, 0:768].astype(WIDE), axis=0, keepdims=True
+    )
+    s.small[0, 3:4, 0:768] = jnp.sum(
+        s.dqkv2[0:128, 1536:2304].astype(WIDE), axis=0, keepdims=True
+    )
+    d_inputs = s.d_mid[...] + norm_back(d_normed, unit_one, scale_one, gain_one[...])
+    grad_ref[...] = d_inputs.astype(LOW)
+    devices = (near(1), near(2), near(4), z_one, z_two)
+
+    def small_send(step):
+        return send(s.small.at[step], s.small_got.at[step], devices[step])
+
+    def small_add(step, copy):
+        copy.wait_recv()
+        s.small[step + 1] = s.small[step] + s.small_got[step]
+
+    small_copy = small_send(0)
+    units[7].make()
+    units[11].pass_on()
+    small_add(0, small_copy)
+    small_copy = small_send(1)
+    units[3].finish()
+    units[4].finish()
+    units[2].z_pair()
+    units[5].z_all()
+    units[6].z_all()
+    units[9].finish()
+    units[8].make()
+    units[7].pass_on()
+    small_add(1, small_copy)
+    small_copy = small_send(2)
+    units[10].finish()
+    units[3].z_pair()
+    units[4].z_pair()
+    units[2].z_all()
+    units[11].finish()
+    units[9].z_pair()
+    units[8].pass_on()
+    small_add(2, small_copy)
+    small_copy = small_send(3)
+    units[7].finish()
+    units[3].z_all()
+    units[4].z_all()
+    units[10].z_pair()
+    units[11].z_pair()
+    units[9].z_all()
+    small_add(3, small_copy)
+    small_copy = small_send(4)
+    units[8].finish()
+    units[7].z_pair()
+    units[10].z_all()
+    units[11].z_all()
+    units[8].z_pair()
+    units[7].z_all()
+    for j in (0, 1, 5, 6, 2, 3, 4):
+        units[j].done()
+    small_add(4, small_copy)
+    narrow = jnp.zeros((8, 96), WIDE)
+    wide = jnp.zeros((1, 384), WIDE)
+    for j in range(8):
+        ours = jnp.where(me == j, 1.0, 0.0)
+        narrow = narrow + ours * s.small[5, :, 96 * j : 96 * j + 96]
+        wide = wide + ours * s.small[5, j : j + 1, 768:1152]
+    small_ref[...] = narrow
+    wide_ref[...] = wide
+    units[8].z_all()
+    for j in (9, 10, 11, 7, 8):
+        units[j].done()
+    for copy in writes:
+        copy.wait()
+    for copy in messages:
+        copy.wait_send()
+
+
+def spread_kernel(total_ref, small_ref, wide_ref, *outs):
+    gain_one, shift_one, qkv, bias_q, bias_v, out, bias_out = outs[:7]
+    gain_two, shift_two, up, bias_up, down, bias_down = outs[7:]
+    for j in range(4):
+        down[96 * j : 96 * j + 96, :] = total_ref[j].astype(WIDE)
+        up[:, 768 * j : 768 * j + 768] = total_ref[5 + j].astype(WIDE)
+    out[...] = total_ref[4].astype(WIDE)
+    for j in range(3):
+        qkv[:, 768 * j : 768 * j + 768] = total_ref[9 + j].astype(WIDE)
+    rows = (gain_one, shift_one, bias_q, bias_v, bias_out, gain_two, shift_two, bias_down)
+    for j, target in enumerate(rows):
+        target[...] = small_ref[j, :]
+    bias_up[...] = wide_ref[0, :]
+
+
+def fused_device(
+    inputs,
+    gain_one,
+    shift_one,
+    w_qkv,
+    bias_q,
+    bias_v,
+    w_out,
+    bias_out,
+    gain_two,
+    shift_two,
+    w_up,
+    bias_up,
+    w_down,
+    bias_down,
+    lengths,
+    cotangent,
+):
+    vmem = pl.BlockSpec(memory_space=pltpu.VMEM)
+    anywhere = pl.BlockSpec(memory_space=pl.ANY)
+    vectors = [gain_one, shift_one, bias_q, bias_v, bias_out, gain_two, shift_two]
+    vectors = [v.reshape(1, -1) for v in vectors + [bias_up, bias_down]]
+    tokens, width = inputs.shape
+    layer_out, grad_inputs, total, small, wide = pl.pallas_call(
+        layer_kernel,
+        out_shape=(
+            jax.ShapeDtypeStruct((tokens, width), LOW),
+            jax.ShapeDtypeStruct((tokens, width), LOW),
+            jax.ShapeDtypeStruct((ROW_UNITS, 2, 48, 768), LOW),
+            jax.ShapeDtypeStruct((8, 96), WIDE),
+            jax.ShapeDtypeStruct((1, 384), WIDE),
+        ),
+        in_specs=[pl.BlockSpec(memory_space=pltpu.SMEM)] + [vmem] * 11 + [anywhere] * 4,
+        out_specs=(vmem, vmem, anywhere, vmem, vmem),
+        scratch_shapes=[pltpu.VMEM(shape, kind) for shape, kind in SCRATCH.values()]
+        + [
+            pltpu.SemaphoreType.DMA((180,)),
+            pltpu.SemaphoreType.DMA((180,)),
+            pltpu.SemaphoreType.DMA((4 + ROW_UNITS,)),
+        ],
+        compiler_params=pltpu.CompilerParams(
+            collective_id=0, has_side_effects=True, vmem_limit_bytes=VMEM_BYTES
+        ),
+        name="layer",
+    )(lengths, inputs, cotangent, *vectors, w_qkv, w_out, w_up, w_down.reshape(32, 96, width))
+    grads = pl.pallas_call(
+        spread_kernel,
+        out_shape=tuple(
+            jax.ShapeDtypeStruct(shape, WIDE)
+            for shape in (
+                (96,),
+                (96,),
+                (96, 2304),
+                (96,),
+                (96,),
+                (96, 768),
+                (96,),
+                (96,),
+                (96,),
+                (96, 3072),
+                (384,),
+                (384, 768),
+                (96,),
+            )
+        ),
+        in_specs=[vmem] * 3,
+        out_specs=(vmem,) * 13,
+        compiler_params=pltpu.CompilerParams(vmem_limit_bytes=VMEM_BYTES),
+        name="spread",
+    )(total.reshape(ROW_UNITS, 96, width), small, wide)
+    return (layer_out, grad_inputs, *grads)
+
+
+VMEM_BYTES = 63 * 2**20
+
+
+def per_device(*arguments):
+    inputs, w_up = arguments[0], arguments[10]
+    fits = (
+        lax.axis_size("dp") == 4
+        and lax.axis_size("col") == 8
+        and inputs.shape == (128, 768)
+        and w_up.shape == (768, 3072)
+    )
+    return fused_device(*arguments) if fits else general_device(*arguments)
+
+
 def solution(mesh):
     return jax.shard_map(
         per_device,

time: 772 us -> 159 us (0.21); the launches traced: 759 us -> 159 us
  waiting for transfers between devices: 317 us -> 0 us
  Pallas kernels: 0 us -> 147 us
  local copies, waits for them, and re-layouts: 154 us -> 11.5 us
  other arithmetic: 116 us -> 0 us
  matrix products: 79.5 us -> 0 us
  blocking collectives: 59.1 us -> 0 us
  between operations: 16.4 us -> 0.69 us
  starting transfers between devices: 13.6 us -> 0 us
    reduce_scatter x5 -> x0, waiting for transfers between devices: 282 us -> none  [the longest x1 78.2 us: per_device(): lax.psum_scatter(grad_w_down, 'col', scatter_dimension=0, tiled=True)]
    pallas_call x0 -> x2, Pallas kernels: none -> 147 us  [the longest x1 143 us: fused_device(): pl.pallas_call(layer_kernel, out_shape=(jax.ShapeDtypeStruct((tokens, wid...]
    dot_general x26 -> x0, matrix products: 79.5 us -> none  [the longest x2 7.64 us: backward_block(): jnp.einsum('khd,qhd->hkq', value_heads, grad_block, preferred_element_typ...]
    unnamed x110 -> x6, local copies, waits for them, and re-layouts: 38.8 us -> 1.36 us
    convert_element_type x21 -> x0, other arithmetic: 31.6 us -> none  [the longest x2 5.24 us: per_device(): got_top, got_total, got_numer = (lax.all_to_all(row_tops[None].astype(jnp...]
    unnamed x1 -> x0, blocking collectives: 26.2 us -> none
    dynamic_update_slice x14 -> x0, local copies, waits for them, and re-layouts: 25.1 us -> none  [per_device(): lax.scan(forward_block, jnp.zeros((tok_rows,), jnp.float32), indices)]
    convert_element_type x11 -> x0, local copies, waits for them, and re-layouts: 23.4 us -> none  [the longest x1 5.49 us: per_device(): numerators[None].astype(jnp.bfloat16)]
  transfers between devices with their start and end apart: 11 -> 0, of which waited for: 9 -> 0; matrix products, arithmetic and copies ran while one was open for 17% -> 0% of each run, Pallas kernels for 0% -> 0%
where the time goes in v1:
time: 159 us
  Pallas kernels  147 us (92%)
  local copies, waits for them, and re-layouts  11.5 us (7%)
    pallas_call x1, Pallas kernels, fused_device(): pl.pallas_call(layer_kernel, out_shape=(jax.ShapeDtypeStruct((tokens, wid...  143 us
    reshape x8, local copies, waits for them, and re-layouts, fused_device(): vectors = [v.reshape(1, -1) for v in vectors + [bias_up, bias_down]]  10.1 us
    pallas_call x1, Pallas kernels, fused_device(): pl.pallas_call(spread_kernel, out_shape=tuple((jax.ShapeDtypeStruct(shape...  3.5 us

profile of v1, /device:TPU:0, one launch (start us, length us, event | category | flops | bytes accessed | tf_op | source)
XLA Modules:
  0.0 159.0 jit_solution(7667533901216576051)
XLA Ops:
  0.6 1.3 reshape.63.gain_one
  1.9 1.3 reshape.64.shift_one
  3.2 1.3 reshape.65.bias_q
  4.4 1.3 reshape.66.bias_v
  5.7 1.3 reshape.67.bias_out
  7.0 1.3 reshape.68.gain_two
  8.2 1.3 reshape.69.shift_two
  9.5 1.3 reshape.71.bias_down
  10.8 143.3 %layer.1 = (bf16[128,768]{1,0:T(8,128)(2,1)}, bf16[128,768]{1,0:T(8,128)(2,1)}, bf16[12,2,48,768]{3,2,1,0:T(8,128)(2,1)}, f32[8,96]{1,0:T(8,128)}, f32[1,384]{1,0:T(1,128)}) custom-call(s32[1,4]{1,0:T(1,128)} %lengths_ref.1, bf16[128,768]{1,0:T(8,128)(2,1)} %x_ref.1, bf16[128,768]{1,0:T(8,128)(2,1)} %cot_ref.1, f32[1,768]{1,0:T(1,128)} %reshape.63.gain_one, ...), custom_call_target="tpu_custom_call" | custom-call | tf_op jit(solution)/shard_map/layer/pallas_call | solution.py:1068
  154.1 0.0 copy-start.1
  154.1 0.0 copy-start
  154.1 3.5 %spread.1 = (f32[96]{0:T(128)}, f32[96]{0:T(128)}, f32[96,2304]{1,0:T(8,128)}, f32[96]{0:T(128)}, f32[96]{0:T(128)}, /*index=5*/f32[96,768]{1,0:T(8,128)}, f32[9...) custom-call(bf16[12,96,768]{2,1,0:T(8,128)(2,1)} %bitcast.4, ...), custom_call_target="tpu_custom_call" | custom-call | tf_op jit(solution)/shard_map/spread/pallas_call | solution.py:1090
  157.6 0.0 copy-done.1
  157.6 0.7 copy.33
  158.3 0.0 copy-done
  158.3 0.7 copy.34
Async XLA Ops:
  154.1 3.5 %copy-start.1 = (bf16[128,768]{1,0:T(8,128)(2,1)S(1)}, bf16[128,768]{1,0:T(8,128)(2,1)}, u32[]{:S(2)}) copy-start(bf16[128,768]{1,0:T(8,128)(2,1)} %get-tuple-element.66) | copy-start | bytes 589828
  154.1 4.2 %copy-start = (bf16[128,768]{1,0:T(8,128)(2,1)S(1)}, bf16[128,768]{1,0:T(8,128)(2,1)}, u32[]{:S(2)}) copy-start(bf16[128,768]{1,0:T(8,128)(2,1)} %get-tuple-element.67) | copy-start | bytes 589828

commit v2 on v0

--- a/solution.py
+++ b/solution.py
@@ -1,6 +1,11 @@
+import functools
+import types
+
 import jax
 import jax.numpy as jnp
 from jax import lax
+from jax.experimental import pallas as pl
+from jax.experimental.pallas import tpu as pltpu
 from jax.sharding import PartitionSpec as P
 
 H = 12
@@ -27,7 +32,7 @@
     return (doc_index, first_place == places)
 
 
-def per_device(
+def general_device(
     inputs,
     gain_one,
     shift_one,
@@ -291,6 +296,872 @@
     )
 
 
+MESH = pl.DeviceIdType.MESH
+LOW = jnp.bfloat16
+WIDE = jnp.float32
+FAR = 1e30
+VMEM_BYTES = 63 * 2**20
+
+
+def dot(a, b):
+    return jnp.dot(a, b, preferred_element_type=WIDE)
+
+
+def dot_rows(a, b):
+    return lax.dot_general(a, b, (((1,), (1,)), ((), ())), preferred_element_type=WIDE)
+
+
+def split_low(values):
+    high = values.astype(LOW)
+    return high, (values - high.astype(WIDE)).astype(LOW)
+
+
+def column_sum(values):
+    return jnp.sum(values.astype(WIDE), axis=0, keepdims=True)
+
+
+def norm_parts(values):
+    average = jnp.mean(values, axis=-1, keepdims=True)
+    centered = values - average
+    spread = jnp.mean(centered * centered, axis=-1, keepdims=True)
+    scale = lax.rsqrt(spread + epsilon)
+    return centered * scale, scale
+
+
+def norm_back(grad, unit, scale, gain):
+    scaled = grad * gain
+    first = jnp.mean(scaled, axis=-1, keepdims=True)
+    second = jnp.mean(scaled * unit, axis=-1, keepdims=True)
+    return scale * (scaled - first - unit * second)
+
+
+def gelu_parts(hidden):
+    square = hidden * hidden
+    bend = jnp.tanh(0.7978845608028654 * hidden * (1.0 + 0.044715 * square))
+    half = 0.5 * (1.0 + bend)
+    curve = 0.7978845608028654 * (1.0 + 3 * 0.044715 * square)
+    return hidden * half, half + 0.5 * hidden * (1.0 - bend * bend) * curve
+
+
+SCRATCH = dict(
+    wqkv=((768, 2304), LOW),
+    wout=((768, 768), LOW),
+    wup=((768, 3072), LOW),
+    wdown=((32, 96, 768), LOW),
+    wup_own=((768, 384), LOW),
+    n1=((8, 128, 768), LOW),
+    n1_t=((8, 96, 1024), LOW),
+    n2=((8, 128, 768), LOW),
+    n2_t=((8, 96, 1024), LOW),
+    cot=((8, 128, 768), LOW),
+    keys=((1024, 768), LOW),
+    values=((1024, 768), LOW),
+    turned=((6, 128, 1024), LOW),
+    probs=((6, 1024, 256), LOW),
+    sums=((8, 8, 128), WIDE),
+    back_sums=((8, 8, 128), WIDE),
+    forgot=((128, 1024), WIDE),
+    forgot_t=((1024, 128), WIDE),
+    sig_t=((1024, 128), WIDE),
+    d_forgot_t=((1024, 128), WIDE),
+    second_head=((1024, 128), LOW),
+    q_low=((128, 768), LOW),
+    q_turned=((768, 128), LOW),
+    att_t=((768, 128), WIDE),
+    att_low_t=((8, 96, 128), LOW),
+    act=((128, 3072), LOW),
+    d_act=((128, 3072), WIDE),
+    d_hidden=((128, 3072), LOW),
+    middle=((128, 768), WIDE),
+    d_mid=((128, 768), WIDE),
+    unit_two=((128, 768), WIDE),
+    d_att=((128, 768), LOW),
+    d_att_t=((768, 128), LOW),
+    dq_t=((768, 128), WIDE),
+    act_t=((384, 1024), LOW),
+    slope=((1024, 384), LOW),
+    db2=((256, 768), LOW),
+    dq2=((256, 768), LOW),
+    lhs_out=((4, 96, 256), LOW),
+    lhs_q=((4, 96, 256), LOW),
+    give_out=((4, 96, 128), LOW),
+    give_q=((4, 96, 128), LOW),
+    dkv=((1024, 1536), LOW),
+    grads_out=((4, 96, 768), LOW),
+    grads_q=((4, 96, 768), LOW),
+    grads_k=((2, 4, 96, 768), LOW),
+    grads_v=((2, 4, 96, 768), LOW),
+    core_k=((4, 96, 768), LOW),
+    core_v=((4, 96, 768), LOW),
+    one=((4, 2, 2, 96, 384), LOW),
+    two=((4, 2, 96, 384), LOW),
+    d_n1=((2, 4, 128, 768), LOW),
+    core_n1=((4, 128, 768), LOW),
+    one_n1=((2, 2, 128, 384), LOW),
+    two_n1=((2, 128, 384), LOW),
+    up_give=((8, 96, 384), LOW),
+    mine=((12, 2, 96, 384), LOW),
+    got_z=((12, 2, 96, 384), LOW),
+    got_mid=((12, 2, 96, 384), LOW),
+    total=((12, 2, 96, 384), LOW),
+    small=((8, 768), WIDE),
+    wide=((8, 384), WIDE),
+    pieces=((8, 16, 128), WIDE),
+    pieces_got=((8, 16, 128), WIDE),
+    rows_z=((4, 16, 128), WIDE),
+)
+SLOTS = (0, 2, 6, 4)
+COPIES = 160
+
+
+def layer_kernel(
+    lengths_ref,
+    x_ref,
+    cot_ref,
+    gain_one,
+    shift_one,
+    bias_q,
+    bias_v,
+    bias_out,
+    gain_two,
+    shift_two,
+    bias_up,
+    bias_down,
+    w_qkv,
+    w_out,
+    w_up,
+    w_down,
+    out_ref,
+    grad_ref,
+    total_ref,
+    small_ref,
+    *scratch,
+):
+    s = types.SimpleNamespace(**dict(zip(SCRATCH, scratch)))
+    gain_one, shift_one, bias_q, bias_v, bias_out, gain_two, shift_two, bias_up, bias_down = (
+        ref[...].reshape(1, -1)
+        for ref in (
+            gain_one,
+            shift_one,
+            bias_q,
+            bias_v,
+            bias_out,
+            gain_two,
+            shift_two,
+            bias_up,
+            bias_down,
+        )
+    )
+    sent, landed, local = scratch[len(SCRATCH) :]
+    me = lax.axis_index("col")
+    dp = lax.axis_index("dp")
+    core = lax.rem(me, 2)
+    x_bit = lax.rem(lax.div(me, 2), 2)
+    y_bit = lax.div(me, 4)
+
+    def place(r):
+        step = (r & 1) * (1 - 2 * core) + ((r >> 1) & 1) * (2 - 4 * x_bit)
+        return me + step + (r >> 2) * (4 - 8 * y_bit)
+
+    def near(r):
+        return (dp, place(r))
+
+    z_pair = (dp + 1 - 2 * lax.rem(dp, 2), me)
+    z_middle = (3 - dp, me)
+    inner = (dp == 1) | (dp == 2)
+    outer = jnp.logical_not(inner)
+    messages = []
+    numbers = iter(range(COPIES))
+
+    def message(source, target, device):
+        at = next(numbers)
+        return pltpu.make_async_remote_copy(
+            src_ref=source,
+            dst_ref=target,
+            send_sem=sent.at[at],
+            recv_sem=landed.at[at],
+            device_id=device,
+            device_id_type=MESH,
+        )
+
+    def send(source, target, device):
+        copy = message(source, target, device)
+        copy.start()
+        messages.append(copy)
+        return copy
+
+    loads = {}
+    for at, (name, source, target) in enumerate(
+        (
+            ("kv", w_qkv.at[:, pl.ds(768, 1536)], s.wqkv.at[:, pl.ds(768, 1536)]),
+            ("q", w_qkv.at[:, pl.ds(0, 768)], s.wqkv.at[:, pl.ds(0, 768)]),
+            ("down", w_down, s.wdown),
+            ("out", w_out, s.wout),
+            ("up", w_up, s.wup),
+            (
+                "own",
+                w_up.at[:, pl.ds(pl.multiple_of(384 * me, 128), 384)],
+                s.wup_own,
+            ),
+        )
+    ):
+        loads[name] = pltpu.make_async_copy(source, target, local.at[at])
+    loads["kv"].start()
+
+    barrier = pltpu.get_barrier_semaphore()
+    others_z = [(lax.rem(dp + k, 4), me) for k in (1, 2, 3)]
+    for device in [near(r) for r in range(1, 8)] + others_z:
+        pl.semaphore_signal(barrier, inc=1, device_id=device, device_id_type=MESH)
+
+    class Gather:
+        def __init__(self, ref):
+            self.ref = ref
+
+        def start(self):
+            self.first = [
+                send(self.ref.at[0], self.ref.at[r], near(r)) for r in (2, 4, 1)
+            ]
+
+        def forward(self):
+            ref = self.ref
+            left, right = pl.ds(0, 384), pl.ds(384, 384)
+            self.first[0].wait_recv()
+            self.far = [send(ref.at[2, :, left], ref.at[6, :, left], near(4))]
+            self.more = [send(ref.at[2], ref.at[3], near(1))]
+            self.first[1].wait_recv()
+            self.far.append(send(ref.at[4, :, right], ref.at[6, :, right], near(2)))
+            self.more.append(send(ref.at[4], ref.at[5], near(1)))
+
+        def diagonal(self):
+            self.far[0].wait_recv()
+            self.far[1].wait_recv()
+            self.more.append(send(self.ref.at[6], self.ref.at[7], near(1)))
+
+        def chip(self, number):
+            (self.first[2] if number == 0 else self.more[number - 1]).wait_recv()
+
+        def rows(self, number):
+            return self.ref[2 * number : 2 * number + 2].reshape(256, 768)
+
+    values_one = x_ref[...].astype(WIDE)
+    unit_one, scale_one = norm_parts(values_one)
+    normed_one = (unit_one * gain_one + shift_one).astype(LOW)
+    s.n1[0] = normed_one
+    s.cot[0] = cot_ref[...]
+    gather_one, gather_cot, gather_two = Gather(s.n1), Gather(s.cot), Gather(s.n2)
+    pl.semaphore_wait(barrier, 10)
+    gather_one.start()
+    loads["q"].start()
+    gather_cot.start()
+
+    def share(source, lhs, give):
+        for slot, r in enumerate(SLOTS):
+            ours = place(r)
+            lhs[slot, :, 0:128] = source(ours)
+            give[slot] = source(ours + 1 - 2 * core)
+        return send(give, lhs.at[:, :, pl.ds(128, 128)], near(1))
+
+    def turn_block(source, target, r):
+        target[:, :, 128 * r : 128 * r + 128] = source[r].T.reshape(8, 96, 128)
+
+    turn_block(s.n1, s.n1_t, 0)
+    share_one = share(lambda at: s.n1_t[at, :, 0:128], s.lhs_q, s.give_q)
+
+    def keys_values(number):
+        rows = gather_one.rows(number)
+        at = 256 * number
+        s.keys[at : at + 256, :] = dot(rows, s.wqkv[:, 768:1536]).astype(LOW)
+        s.values[at : at + 256, :] = (dot(rows, s.wqkv[:, 1536:2304]) + bias_v).astype(LOW)
+
+    loads["kv"].wait()
+    loads["down"].start()
+    loads["out"].start()
+    gather_one.chip(0)
+    keys_values(0)
+    loads["q"].wait()
+    loads["up"].start()
+    loads["own"].start()
+    q = (dot(normed_one, s.wqkv[:, 0:768]) + bias_q).astype(LOW)
+    q = (q.astype(WIDE) * 0.125).astype(LOW)
+    s.q_low[...] = q
+    s.q_turned[...] = q.T
+    gather_one.forward()
+    turn_block(s.n1, s.n1_t, 1)
+
+    row_at = lax.broadcasted_iota(jnp.int32, (128, 128), 0)
+    lane_at = lax.broadcasted_iota(jnp.int32, (128, 128), 1)
+    query_at = row_at + me * 128
+    begin_one = lengths_ref[0, 0]
+    begin_two = begin_one + lengths_ref[0, 1]
+    begin_three = begin_two + lengths_ref[0, 2]
+    begin = jnp.where(query_at >= begin_one, begin_one, 0)
+    begin = jnp.where(query_at >= begin_two, begin_two, begin)
+    begin = jnp.where(query_at >= begin_three, begin_three, begin)
+    earlier = jnp.where(lane_at < row_at, 1.0, 0.0).astype(LOW)
+    first_lanes = jnp.where(lane_at < 64, 1.0, 0.0)
+    head_zero = (s.q_low[:, 0:128].astype(WIDE) * first_lanes).astype(LOW)
+
+    def picks(r):
+        scores = dot_rows(head_zero, s.keys[128 * r : 128 * r + 128, 0:128])
+        key_at = lane_at + place(r) * 128
+        allowed = (key_at <= query_at) & (key_at >= begin)
+        chosen = (key_at < query_at) & (key_at > begin)
+        small_exp = jnp.exp(-jnp.abs(scores))
+        soft = jnp.maximum(scores, 0.0) + jnp.log1p(small_exp)
+        picked = jnp.where(chosen, soft, 0.0) * (1.0 / 1024)
+        high, rest = split_low(picked)
+        s.sums[0, r : r + 1, :] = column_sum(picked)
+        within = dot(earlier, high) + dot(earlier, rest)
+        s.forgot[:, 128 * r : 128 * r + 128] = jnp.where(allowed, within, FAR)
+        sigmoid = jnp.where(scores >= 0, 1.0, small_exp) / (1.0 + small_exp)
+        s.sig_t[128 * r : 128 * r + 128, :] = (jnp.where(chosen, sigmoid, 0.0) * (1.0 / 1024)).T
+
+    def turn(source, pair):
+        at = 128 * pair
+        for r in range(8):
+            rows = slice(128 * r, 128 * r + 128)
+            s.turned[pair, :, rows] = source[rows, at : at + 128].T
+
+    for number in (0, 1, 2, 3):
+        if number:
+            gather_one.chip(number)
+            keys_values(number)
+        if number == 1:
+            gather_one.diagonal()
+        picks(2 * number)
+        picks(2 * number + 1)
+        if number:
+            turn_block(s.n1, s.n1_t, 2 * number)
+            turn_block(s.n1, s.n1_t, 2 * number + 1)
+    sum_copies = [send(s.sums.at[0], s.sums.at[r], near(r)) for r in range(1, 8)]
+
+    def active_grad(first, last):
+        for j in range(first, last):
+            rows = s.wdown[4 * j : 4 * j + 4].reshape(384, 768)
+            s.d_act[:, 384 * j : 384 * j + 384] = dot_rows(cot_ref[...], rows)
+
+    loads["down"].wait()
+    active_grad(0, 8)
+    gather_cot.forward()
+    for pair in range(6):
+        turn(s.values, pair)
+    for copy in sum_copies:
+        copy.wait_recv()
+
+    def others(sums, later):
+        rows = [jnp.zeros((1, 128), WIDE) for _ in range(8)]
+        for d in range(1, 8):
+            ahead = place(d) > me if later else place(d) < me
+            weight = jnp.where(ahead, 1.0, 0.0)
+            for r in range(8):
+                rows[r] = rows[r] + weight * sums[d, (r ^ d) : (r ^ d) + 1, :]
+        return rows
+
+    for r, row in enumerate(others(s.sums, False)):
+        at = 128 * r
+        s.forgot_t[at : at + 128, :] = (s.forgot[:, at : at + 128] + row).T
+
+    feature_at = lax.broadcasted_iota(jnp.int32, (128, 256), 0)
+    column_at = lax.broadcasted_iota(jnp.int32, (128, 256), 1)
+    own_head_t = jnp.where((feature_at < 64) == (column_at < 128), 1.0, 0.0).astype(LOW)
+    long_row = lax.broadcasted_iota(jnp.int32, (256, 128), 0)
+    long_lane = lax.broadcasted_iota(jnp.int32, (256, 128), 1)
+    own_head = jnp.where((long_row < 128) == (long_lane < 64), 1.0, 0.0).astype(LOW)
+
+    def both_t(values):
+        return jnp.concatenate([values, values], axis=1) * own_head_t
+
+    def both(values):
+        return jnp.concatenate([values, values], axis=0) * own_head
+
+    def attend(pair):
+        at = 128 * pair
+        scores = dot(s.keys[:, at : at + 128], both_t(s.q_turned[at : at + 128, :]))
+        forgot = s.forgot_t[...]
+        logits = scores - jnp.concatenate([forgot, forgot], axis=1)
+        raised = jnp.exp(logits - jnp.max(logits, axis=0, keepdims=True))
+        probs = (raised * (1.0 / jnp.sum(raised, axis=0, keepdims=True))).astype(LOW)
+        s.probs[pair] = probs
+        mixed = dot(s.turned[pair], probs)
+        s.att_t[at : at + 64, :] = mixed[0:64, 0:128]
+        s.att_t[at + 64 : at + 128, :] = mixed[64:128, 128:256]
+
+    for pair in range(6):
+        attend(pair)
+
+    attended_low_t = s.att_t[...].astype(LOW)
+    s.att_low_t[...] = attended_low_t.reshape(8, 96, 128)
+    loads["out"].wait()
+    middle = values_one + dot(attended_low_t.T, s.wout[...]) + bias_out
+    s.middle[...] = middle
+    unit_two, scale_two = norm_parts(middle)
+    s.unit_two[...] = unit_two
+    normed_two = (unit_two * gain_two + shift_two).astype(LOW)
+    s.n2[0] = normed_two
+    gather_two.start()
+    share_att = share(lambda at: s.att_low_t[at], s.lhs_out, s.give_out)
+    gather_cot.diagonal()
+    loads["up"].wait()
+    for j in range(4):
+        at = 768 * j
+        hidden = dot(normed_two, s.wup[:, at : at + 768]) + bias_up[:, at : at + 768]
+        active, slope = gelu_parts(hidden)
+        s.act[:, at : at + 768] = active.astype(LOW)
+        d_hidden = (s.d_act[:, at : at + 768] * slope).astype(LOW)
+        s.d_hidden[:, at : at + 768] = d_hidden
+        s.wide[2 * j : 2 * j + 1, :] = column_sum(d_hidden[:, 0:384])
+        s.wide[2 * j + 1 : 2 * j + 2, :] = column_sum(d_hidden[:, 384:768])
+    gather_two.forward()
+
+    d_output = cot_ref[...].astype(WIDE)
+    parts = []
+    for j in range(3):
+        parts.append(dot_rows(s.d_hidden[...], s.wup[256 * j : 256 * j + 256, :]))
+    d_normed = jnp.concatenate(parts, axis=1)
+    unit_two = s.unit_two[...]
+    s.small[5:6, :] = column_sum(d_normed * unit_two)
+    s.small[6:7, :] = column_sum(d_normed)
+    s.small[7:8, :] = column_sum(d_output)
+    d_middle = d_output + norm_back(d_normed, unit_two, scale_two, gain_two)
+    s.d_mid[...] = d_middle
+    s.small[4:5, :] = column_sum(d_middle)
+    d_branch = d_middle.astype(LOW)
+    s.db2[0:128, :] = d_branch
+    share_branch = send(s.db2.at[pl.ds(0, 128)], s.db2.at[pl.ds(128, 128)], near(1))
+    d_att_t = dot(s.wout[...], d_branch.T).astype(LOW)
+    s.d_att_t[...] = d_att_t
+    s.d_att[...] = d_att_t.T
+    gather_two.diagonal()
+
+    class Unit:
+        def __init__(self, rows, grads, one, two, core=None):
+            self.rows, self.grads, self.one, self.two, self.core = rows, grads, one, two, core
+
+        def across(self):
+            self.copy = send(self.grads.at[1], self.core, near(1))
+            self.grads = self.grads.at[0]
+
+        def start(self):
+            if self.core is not None:
+                self.copy.wait_recv()
+                total = self.grads[...].astype(WIDE) + self.core[...].astype(WIDE)
+                self.grads[...] = total.astype(LOW)
+            self.copies = (
+                send(self.grads.at[pl.ds(1, 2), :, pl.ds(0, 384)], self.one.at[0], near(2)),
+                send(self.grads.at[pl.ds(2, 2), :, pl.ds(384, 384)], self.one.at[1], near(4)),
+            )
+
+        def pass_on(self):
+            copies = []
+            for half, slot, index, r in ((0, 3, 1, 4), (1, 1, 0, 2)):
+                cols = slice(384 * half, 384 * half + 384)
+                self.copies[half].wait_recv()
+                total = self.grads[slot, :, cols].astype(WIDE)
+                total = total + self.one[half, index].astype(WIDE)
+                self.grads[slot, :, cols] = total.astype(LOW)
+                source = self.grads.at[slot, :, pl.ds(384 * half, 384)]
+                copies.append(send(source, self.two.at[half], near(r)))
+            self.copies = copies
+
+        def finish(self, half):
+            self.copies[half].wait_recv()
+            total = self.grads[0, :, 384 * half : 384 * half + 384].astype(WIDE)
+            total = total + self.one[half, half].astype(WIDE)
+            return total + self.two[half].astype(WIDE)
+
+    class Line:
+        def __init__(self, at, places):
+            self.at, self.places = at, places
+            mine, total = s.mine.at[at], s.total.at[at]
+            self.inward = message(mine, s.got_z.at[at], z_pair)
+            self.across = message(mine, s.got_mid.at[at], z_middle)
+            self.outward = message(total, total, z_pair)
+
+        def start(self):
+            pl.when(outer)(lambda: self.inward.start())
+
+        def middle(self):
+            @pl.when(inner)
+            def _():
+                self.inward.wait_recv()
+                total = s.mine[self.at].astype(WIDE) + s.got_z[self.at].astype(WIDE)
+                s.mine[self.at] = total.astype(LOW)
+                self.across.start()
+
+        def back(self):
+            @pl.when(inner)
+            def _():
+                self.across.wait_recv()
+                total = s.mine[self.at].astype(WIDE) + s.got_mid[self.at].astype(WIDE)
+                s.total[self.at] = total.astype(LOW)
+                self.outward.start()
+
+        def write(self):
+            pl.when(outer)(lambda: self.outward.wait_recv())
+            for i, where in enumerate(self.places):
+                copy = pltpu.make_async_copy(
+                    s.total.at[self.at, i], total_ref.at[where], local.at[6 + 2 * self.at + i]
+                )
+                copy.start()
+                writes.append(copy)
+
+        def close(self):
+            pl.when(outer)(lambda: self.inward.wait_send())
+
+            @pl.when(inner)
+            def _():
+                self.across.wait_send()
+                self.outward.wait_send()
+
+    writes = []
+    lines = [Line(j, (2 * j, 2 * j + 1)) for j in range(5)]
+    lines += [Line(5 + j, (10 + place(2 * j), 10 + place(2 * j + 1))) for j in range(4)]
+    lines += [Line(9 + j, (18 + 2 * j, 19 + 2 * j)) for j in range(3)]
+    unit_out = Unit(96, s.grads_out, s.one.at[0], s.two.at[0])
+    unit_q = Unit(96, s.grads_q, s.one.at[1], s.two.at[1])
+    unit_k = Unit(96, s.grads_k, s.one.at[2], s.two.at[2], s.core_k)
+    unit_v = Unit(96, s.grads_v, s.one.at[3], s.two.at[3], s.core_v)
+    unit_n1 = Unit(128, s.d_n1, s.one_n1, s.two_n1, s.core_n1)
+
+    def to_line(unit, at):
+        for half in range(2):
+            s.mine[at, half] = unit.finish(half).astype(LOW)
+        lines[at].start()
+
+    def rows_of(source, odd):
+        return jnp.concatenate([source[place(r + odd)] for r in SLOTS], axis=0)
+
+    own_down = s.wdown.at[pl.ds(4 * me, 4)]
+    own_bias = jnp.zeros((1, 384), WIDE)
+    for j in range(8):
+        own_bias = own_bias + jnp.where(me == j, 1.0, 0.0) * bias_up[:, 384 * j : 384 * j + 384]
+    loads["own"].wait()
+
+    def own_units(number):
+        gather_cot.chip(number)
+        gather_two.chip(number)
+        at = 256 * number
+        hidden = dot(gather_two.rows(number), s.wup_own[...]) + own_bias
+        active, slope = gelu_parts(hidden)
+        d_active = dot_rows(gather_cot.rows(number), own_down[...].reshape(384, 768))
+        s.act_t[:, at : at + 256] = active.astype(LOW).T
+        s.slope[at : at + 256, :] = (d_active * slope).astype(LOW)
+        turn_block(s.n2, s.n2_t, 2 * number)
+        turn_block(s.n2, s.n2_t, 2 * number + 1)
+
+    for number in range(4):
+        own_units(number)
+    share_att.wait_recv()
+    share_branch.wait_recv()
+    s.grads_out[...] = (
+        dot(s.lhs_out[...].reshape(384, 256), s.db2[...]).astype(LOW).reshape(4, 96, 768)
+    )
+    unit_out.start()
+    cot_rows = s.cot[...].reshape(1024, 768)
+    for j in range(4):
+        grads = dot(s.act_t[96 * j : 96 * j + 96, :], cot_rows).astype(LOW)
+        s.mine[j, 0] = grads[:, 0:384]
+        s.mine[j, 1] = grads[:, 384:768]
+        lines[j].start()
+    up_copies = []
+    for odd in range(2):
+        grads = dot(rows_of(s.n2_t, odd), s.slope[...]).astype(LOW).reshape(4, 96, 384)
+        for slot, r in enumerate(SLOTS):
+            if r + odd == 0:
+                s.mine[5, 0] = grads[0]
+            else:
+                s.up_give[r + odd] = grads[slot]
+                target = s.mine.at[5 + r // 2, odd]
+                up_copies.append(send(s.up_give.at[r + odd], target, near(r + odd)))
+
+    def logit_grads(pair):
+        at = 128 * pair
+        grad_t = s.d_att_t[at : at + 128, :]
+        products = grad_t.astype(WIDE) * s.att_t[at : at + 128, :]
+        delta = jnp.concatenate(
+            [
+                jnp.sum(products[0:64], axis=0, keepdims=True),
+                jnp.sum(products[64:128], axis=0, keepdims=True),
+            ],
+            axis=1,
+        )
+        d_probs = dot(s.values[:, at : at + 128], both_t(grad_t))
+        d_logits = s.probs[pair].astype(WIDE) * (d_probs - delta)
+        both_heads = d_logits[:, 0:128] + d_logits[:, 128:256]
+        if pair == 5:
+            s.d_forgot_t[...] = both_heads
+        else:
+            s.d_forgot_t[...] += both_heads
+        return d_logits
+
+    def value_grads(pair):
+        at = 128 * pair
+        grads = dot(s.probs[pair], both(s.d_att[:, at : at + 128]))
+        s.dkv[:, 768 + at : 896 + at] = grads.astype(LOW)
+
+    def score_grads(pair, d_scores):
+        at = 128 * pair
+        turn(s.keys, pair)
+        s.dkv[:, at : at + 128] = dot(d_scores, both(s.q_low[:, at : at + 128])).astype(LOW)
+        grads = dot(s.turned[pair], d_scores)
+        s.dq_t[at : at + 64, :] = grads[0:64, 0:128]
+        s.dq_t[at + 64 : at + 128, :] = grads[64:128, 128:256]
+
+    def attend_back(pair):
+        d_logits = logit_grads(pair)
+        value_grads(pair)
+        score_grads(pair, d_logits.astype(LOW))
+
+    attend_back(5)
+    lines[0].middle()
+    attend_back(4)
+    lines[1].middle()
+    attend_back(3)
+    unit_out.pass_on()
+    lines[2].middle()
+    attend_back(2)
+    lines[0].back()
+    lines[3].middle()
+    attend_back(1)
+    d_logits = logit_grads(0)
+    s.forgot_t[...] = d_logits[:, 0:128]
+    s.second_head[...] = d_logits[:, 128:256].astype(LOW)
+    for r in range(8):
+        turned = s.d_forgot_t[128 * r : 128 * r + 128, :].T
+        s.back_sums[0, r : r + 1, :] = column_sum(turned)
+    sum_copies = [send(s.back_sums.at[0], s.back_sums.at[r], near(r)) for r in range(1, 8)]
+    value_grads(0)
+    lines[1].back()
+    to_line(unit_out, 4)
+
+    def key_unit(unit, half):
+        grads = s.dkv[:, 768 * half : 768 * half + 768]
+        for odd in (1, 0):
+            rows = rows_of(s.n1_t, odd)
+            unit.grads[odd] = dot(rows, grads).astype(LOW).reshape(4, 96, 768)
+        unit.across()
+
+    key_unit(unit_v, 1)
+    for copy in up_copies:
+        copy.wait_recv()
+    for j in range(4):
+        lines[5 + j].start()
+    for copy in sum_copies:
+        copy.wait_recv()
+    later_rows = others(s.back_sums, True)
+    following = jnp.where(row_at > lane_at, 1.0, 0.0).astype(LOW)
+    selected = []
+    for r in range(8):
+        at = 128 * r
+        high, rest = split_low(s.d_forgot_t[at : at + 128, :])
+        later = jnp.broadcast_to(later_rows[r], (128, 128)).T
+        d_picked = -(dot(high, following) + dot(rest, following) + later)
+        selected.append(s.forgot_t[at : at + 128, :] + s.sig_t[at : at + 128, :] * d_picked)
+    first_head = jnp.concatenate(selected, axis=0).astype(LOW)
+    score_grads(0, jnp.concatenate([first_head, s.second_head[...]], axis=1))
+    for j in range(6):
+        at = 128 * j
+        d_q = (s.dq_t[at : at + 128, :] * 0.125).astype(LOW)
+        s.dq2[0:128, at : at + 128] = d_q.T
+    share_q = send(s.dq2.at[pl.ds(0, 128)], s.dq2.at[pl.ds(128, 128)], near(1))
+    unit_v.start()
+    lines[2].back()
+    key_unit(unit_k, 0)
+    lines[3].back()
+    lines[4].middle()
+    lines[5].middle()
+    share_one.wait_recv()
+    share_q.wait_recv()
+    s.grads_q[...] = (
+        dot(s.lhs_q[...].reshape(384, 256), s.dq2[...]).astype(LOW).reshape(4, 96, 768)
+    )
+    unit_q.start()
+    unit_k.start()
+    unit_v.pass_on()
+    lines[6].middle()
+    lines[4].back()
+    for slot, r in enumerate(SLOTS):
+        for odd in range(2):
+            at = 128 * (r + odd)
+            for j in range(3):
+                cols = slice(256 * j, 256 * j + 256)
+                grads = dot_rows(s.dkv[at : at + 128, :], s.wqkv[cols, 768:2304])
+                s.d_n1[odd, slot, :, cols] = grads.astype(LOW)
+    unit_n1.across()
+    lines[7].middle()
+    lines[5].back()
+    unit_q.pass_on()
+    unit_n1.start()
+    to_line(unit_v, 11)
+    lines[8].middle()
+    lines[6].back()
+    unit_k.pass_on()
+    mixed = jnp.zeros((128, 768), WIDE)
+    for j in range(4):
+        rows = s.wdown[8 * j : 8 * j + 8].reshape(768, 768)
+        mixed = mixed + dot(s.act[:, 768 * j : 768 * j + 768], rows)
+    out_ref[...] = (s.middle[...] + mixed + bias_down).astype(LOW)
+    parts = []
+    for i in range(3):
+        rows = s.wqkv[256 * i : 256 * i + 256, 0:768]
+        parts.append(dot_rows(s.dq2[0:128, :], rows))
+    d_normed = jnp.concatenate(parts, axis=1)
+    to_line(unit_q, 9)
+    lines[11].middle()
+    lines[7].back()
+    unit_n1.pass_on()
+    to_line(unit_k, 10)
+    lines[8].back()
+    lines[9].middle()
+    lines[11].back()
+    for j in (0, 1, 2, 3, 4, 5, 6):
+        lines[j].write()
+    d_normed = d_normed + jnp.concatenate([unit_n1.finish(0), unit_n1.finish(1)], axis=1)
+    unit_one, scale_one = norm_parts(x_ref[...].astype(WIDE))
+    s.small[0:1, :] = column_sum(d_normed * unit_one)
+    s.small[1:2, :] = column_sum(d_normed)
+    s.small[2:3, :] = column_sum(s.dq2[0:128, :])
+    s.small[3:4, :] = column_sum(s.dkv[:, 768:1536])
+    d_inputs = s.d_mid[...] + norm_back(d_normed, unit_one, scale_one, gain_one)
+    grad_ref[...] = d_inputs.astype(LOW)
+
+    s.pieces[...] = jnp.zeros((8, 16, 128), WIDE)
+    for j in range(8):
+        s.pieces[j, 0:8, 0:96] = s.small[:, 96 * j : 96 * j + 96]
+        for i in range(3):
+            s.pieces[j, 8 + i : 9 + i, :] = s.wide[j : j + 1, 128 * i : 128 * i + 128]
+    piece_copies = [
+        send(s.pieces.at[place(r)], s.pieces_got.at[r], near(r)) for r in range(1, 8)
+    ]
+    lines[10].middle()
+    lines[9].back()
+    total = s.pieces[me]
+    for r in range(1, 8):
+        piece_copies[r - 1].wait_recv()
+        total = total + s.pieces_got[r]
+    s.rows_z[dp] = total
+    z_copies = [send(s.rows_z.at[dp], s.rows_z.at[dp], device) for device in others_z]
+    lines[10].back()
+    for j in (7, 8, 11, 9):
+        lines[j].write()
+    for copy in z_copies:
+        copy.wait_recv()
+    small_ref[...] = s.rows_z[0] + s.rows_z[1] + s.rows_z[2] + s.rows_z[3]
+    lines[10].write()
+    for copy in writes:
+        copy.wait()
+    for copy in messages:
+        copy.wait_send()
+    for line in lines:
+        line.close()
+
+
+def spread_kernel(total_ref, small_ref, out_in, grad_in, out_ref, grad_ref, *outs):
+    gain_one, shift_one, qkv, bias_q, bias_v, out, bias_out = outs[:7]
+    gain_two, shift_two, up, bias_up, down, bias_down = outs[7:]
+    out_ref[...] = out_in[...]
+    grad_ref[...] = grad_in[...]
+    for i in range(2):
+        cols = slice(384 * i, 384 * i + 384)
+        for j in range(4):
+            down[96 * j : 96 * j + 96, cols] = total_ref[2 * j + i].astype(WIDE)
+        out[:, cols] = total_ref[8 + i].astype(WIDE)
+    for j in range(8):
+        up[:, 384 * j : 384 * j + 384] = total_ref[10 + j].astype(WIDE)
+    for j in range(6):
+        qkv[:, 384 * j : 384 * j + 384] = total_ref[18 + j].astype(WIDE)
+    rows = (gain_one, shift_one, bias_q, bias_v, bias_out, gain_two, shift_two, bias_down)
+    for j, target in enumerate(rows):
+        target[...] = small_ref[j, 0:96]
+    for i in range(3):
+        bias_up[128 * i : 128 * i + 128] = small_ref[8 + i, :]
+
+
+def fused_device(
+    inputs,
+    gain_one,
+    shift_one,
+    w_qkv,
+    bias_q,
+    bias_v,
+    w_out,
+    bias_out,
+    gain_two,
+    shift_two,
+    w_up,
+    bias_up,
+    w_down,
+    bias_down,
+    lengths,
+    cotangent,
+):
+    vmem = pl.BlockSpec(memory_space=pltpu.VMEM)
+    anywhere = pl.BlockSpec(memory_space=pl.ANY)
+    vectors = [gain_one, shift_one, bias_q, bias_v, bias_out, gain_two, shift_two]
+    vectors = vectors + [bias_up, bias_down]
+    tokens, width = inputs.shape
+    layer_out, grad_inputs, total, small = pl.pallas_call(
+        layer_kernel,
+        out_shape=(
+            jax.ShapeDtypeStruct((tokens, width), LOW),
+            jax.ShapeDtypeStruct((tokens, width), LOW),
+            jax.ShapeDtypeStruct((24, 96, 384), LOW),
+            jax.ShapeDtypeStruct((16, 128), WIDE),
+        ),
+        in_specs=[pl.BlockSpec(memory_space=pltpu.SMEM)] + [vmem] * 11 + [anywhere] * 4,
+        out_specs=(vmem, vmem, anywhere, vmem),
+        scratch_shapes=[pltpu.VMEM(shape, kind) for shape, kind in SCRATCH.values()]
+        + [
+            pltpu.SemaphoreType.DMA((COPIES,)),
+            pltpu.SemaphoreType.DMA((COPIES,)),
+            pltpu.SemaphoreType.DMA((30,)),
+        ],
+        compiler_params=pltpu.CompilerParams(
+            collective_id=0, has_side_effects=True, vmem_limit_bytes=VMEM_BYTES
+        ),
+        name="layer",
+    )(lengths, inputs, cotangent, *vectors, w_qkv, w_out, w_up, w_down.reshape(32, 96, width))
+    return pl.pallas_call(
+        spread_kernel,
+        out_shape=tuple(
+            jax.ShapeDtypeStruct((tokens, width), LOW) for _ in range(2)
+        )
+        + tuple(
+            jax.ShapeDtypeStruct(shape, WIDE)
+            for shape in (
+                (96,),
+                (96,),
+                (96, 2304),
+                (96,),
+                (96,),
+                (96, 768),
+                (96,),
+                (96,),
+                (96,),
+                (96, 3072),
+                (384,),
+                (384, 768),
+                (96,),
+            )
+        ),
+        in_specs=[vmem] * 4,
+        out_specs=(vmem,) * 15,
+        compiler_params=pltpu.CompilerParams(vmem_limit_bytes=VMEM_BYTES),
+        name="spread",
+    )(total, small, layer_out, grad_inputs)
+
+
+def per_device(*arguments):
+    inputs, w_up = arguments[0], arguments[10]
+    fits = (
+        lax.axis_size("dp") == 4
+        and lax.axis_size("col") == 8
+        and inputs.shape == (128, 768)
+        and w_up.shape == (768, 3072)
+    )
+    return fused_device(*arguments) if fits else general_device(*arguments)
+
+
 def solution(mesh):
     return jax.shard_map(
         per_device,

time: 772 us -> 112 us (0.15); the launches traced: 759 us -> 111 us
  waiting for transfers between devices: 317 us -> 0 us
  local copies, waits for them, and re-layouts: 154 us -> 0 us
  other arithmetic: 116 us -> 0 us
  Pallas kernels: 0 us -> 111 us
  matrix products: 79.5 us -> 0 us
  blocking collectives: 59.1 us -> 0 us
  between operations: 16.4 us -> 0.84 us
  starting transfers between devices: 13.6 us -> 0 us
    reduce_scatter x5 -> x0, waiting for transfers between devices: 282 us -> none  [the longest x1 78.2 us: per_device(): lax.psum_scatter(grad_w_down, 'col', scatter_dimension=0, tiled=True)]
    pallas_call x0 -> x2, Pallas kernels: none -> 111 us  [the longest x1 107 us: fused_device(): pl.pallas_call(layer_kernel, out_shape=(jax.ShapeDtypeStruct((tokens, wid...]
    dot_general x26 -> x0, matrix products: 79.5 us -> none  [the longest x2 7.64 us: backward_block(): jnp.einsum('khd,qhd->hkq', value_heads, grad_block, preferred_element_typ...]
    unnamed x110 -> x0, local copies, waits for them, and re-layouts: 38.8 us -> none
    convert_element_type x21 -> x0, other arithmetic: 31.6 us -> none  [the longest x2 5.24 us: per_device(): got_top, got_total, got_numer = (lax.all_to_all(row_tops[None].astype(jnp...]
    unnamed x1 -> x0, blocking collectives: 26.2 us -> none
    dynamic_update_slice x14 -> x0, local copies, waits for them, and re-layouts: 25.1 us -> none  [per_device(): lax.scan(forward_block, jnp.zeros((tok_rows,), jnp.float32), indices)]
    convert_element_type x11 -> x0, local copies, waits for them, and re-layouts: 23.4 us -> none  [the longest x1 5.49 us: per_device(): numerators[None].astype(jnp.bfloat16)]
  transfers between devices with their start and end apart: 11 -> 0, of which waited for: 9 -> 0; matrix products, arithmetic and copies ran while one was open for 17% -> 0% of each run, Pallas kernels for 0% -> 0%
where the time goes in v2:
time: 112 us; the launch traced here: 111 us
  Pallas kernels  111 us (99%)
    pallas_call x1, Pallas kernels, fused_device(): pl.pallas_call(layer_kernel, out_shape=(jax.ShapeDtypeStruct((tokens, wid...  107 us
    pallas_call x1, Pallas kernels, fused_device(): pl.pallas_call(spread_kernel, out_shape=tuple((jax.ShapeDtypeStruct((toke...  3.55 us

profile of v2, /device:TPU:0, one launch (start us, length us, event | category | flops | bytes accessed | tf_op | source)
XLA Modules:
  0.0 111.4 jit_solution(9498084045944626323)
XLA Ops:
  0.7 107.1 %layer.1 = (bf16[128,768]{1,0:T(8,128)(2,1)}, bf16[128,768]{1,0:T(8,128)(2,1)}, bf16[24,96,384]{2,1,0:T(8,128)(2,1)}, f32[16,128]{1,0:T(8,128)}) custom-call(s32[1,4]{1,0:T(1,128)} %lengths_ref.1, bf16[128,768]{1,0:T(8,128)(2,1)} %x_ref.1, bf16[128,768]{1,0:T(8,128)(2,1)} %cot_ref.1, f32[768]{0:T(1024)} %gain_one.1, f32[768]{0:T(1024)} %shift_one.1, ...), custom_call_target="tpu_custom_call" | custom-call | tf_op jit(solution)/shard_map/layer/pallas_call | solution.py:1103
  107.7 3.6 %spread.1 = (bf16[128,768]{1,0:T(8,128)(2,1)}, bf16[128,768]{1,0:T(8,128)(2,1)}, f32[96]{0:T(128)}, f32[96]{0:T(128)}, f32[96,2304]{1,0:T(8,128)}, /*index=5*/f3...) custom-call(bf16[24,96,384]{2,1,0:T(8,128)(2,1)} %get-tuple-element., ...), custom_call_target="tpu_custom_call" | custom-call | tf_op jit(solution)/shard_map/spread/pallas_call | solution.py:1124

commit v3 on v2

--- a/solution.py
+++ b/solution.py
@@ -400,10 +400,10 @@
     one_n1=((2, 2, 128, 384), LOW),
     two_n1=((2, 128, 384), LOW),
     up_give=((8, 96, 384), LOW),
-    mine=((12, 2, 96, 384), LOW),
-    got_z=((12, 2, 96, 384), LOW),
-    got_mid=((12, 2, 96, 384), LOW),
-    total=((12, 2, 96, 384), LOW),
+    mine=((24, 96, 384), LOW),
+    got_z=((24, 96, 384), LOW),
+    got_mid=((24, 96, 384), LOW),
+    total=((24, 96, 384), LOW),
     small=((8, 768), WIDE),
     wide=((8, 384), WIDE),
     pieces=((8, 16, 128), WIDE),
@@ -411,7 +411,9 @@
     rows_z=((4, 16, 128), WIDE),
 )
 SLOTS = (0, 2, 6, 4)
-COPIES = 160
+RING = 24
+LINES = 12
+LANDINGS = 72
 
 
 def layer_kernel(
@@ -470,27 +472,34 @@
     z_middle = (3 - dp, me)
     inner = (dp == 1) | (dp == 2)
     outer = jnp.logical_not(inner)
-    messages = []
-    numbers = iter(range(COPIES))
-
-    def message(source, target, device):
-        at = next(numbers)
+    landings = iter(range(LANDINGS))
+    ring = [None] * RING
+    turns = iter(range(10**6))
+
+    def message(source, target, device, send_at, land_at):
         return pltpu.make_async_remote_copy(
             src_ref=source,
             dst_ref=target,
-            send_sem=sent.at[at],
-            recv_sem=landed.at[at],
+            send_sem=sent.at[send_at],
+            recv_sem=landed.at[land_at],
             device_id=device,
             device_id_type=MESH,
         )
 
+    def send_all(copies, whole):
+        send_at, land_at = next(turns) % RING, next(landings)
+        if ring[send_at] is not None:
+            ring[send_at].wait_send()
+        for source, target, device in copies:
+            message(source, target, device, send_at, land_at).start()
+        ring[send_at] = message(whole, whole, near(1), send_at, land_at)
+        return ring[send_at]
+
     def send(source, target, device):
-        copy = message(source, target, device)
-        copy.start()
-        messages.append(copy)
-        return copy
+        return send_all([(source, target, device)], source)
 
     loads = {}
+    own_cols = pl.ds(pl.multiple_of(384 * me, 128), 384)
     for at, (name, source, target) in enumerate(
         (
             ("kv", w_qkv.at[:, pl.ds(768, 1536)], s.wqkv.at[:, pl.ds(768, 1536)]),
@@ -498,15 +507,11 @@
             ("down", w_down, s.wdown),
             ("out", w_out, s.wout),
             ("up", w_up, s.wup),
-            (
-                "own",
-                w_up.at[:, pl.ds(pl.multiple_of(384 * me, 128), 384)],
-                s.wup_own,
-            ),
+            ("own", w_up.at[:, own_cols], s.wup_own),
         )
     ):
         loads[name] = pltpu.make_async_copy(source, target, local.at[at])
-    loads["kv"].start()
+        loads[name].start()
 
     barrier = pltpu.get_barrier_semaphore()
     others_z = [(lax.rem(dp + k, 4), me) for k in (1, 2, 3)]
@@ -516,29 +521,40 @@
     class Gather:
         def __init__(self, ref):
             self.ref = ref
+            self.left, self.right = pl.ds(0, 384), pl.ds(384, 384)
 
         def start(self):
-            self.first = [
-                send(self.ref.at[0], self.ref.at[r], near(r)) for r in (2, 4, 1)
-            ]
+            ref, own = self.ref, self.ref.at[0]
+            pair = []
+            for first, second in ((self.left, self.right), (self.right, self.left)):
+                copies = [
+                    (own.at[:, first], ref.at[2, :, first], near(2)),
+                    (own.at[:, second], ref.at[4, :, second], near(4)),
+                ]
+                pair.append(send_all(copies, own))
+            self.early, self.late = pair
+            self.other = send(own, ref.at[1], near(1))
 
         def forward(self):
             ref = self.ref
-            left, right = pl.ds(0, 384), pl.ds(384, 384)
-            self.first[0].wait_recv()
-            self.far = [send(ref.at[2, :, left], ref.at[6, :, left], near(4))]
-            self.more = [send(ref.at[2], ref.at[3], near(1))]
-            self.first[1].wait_recv()
-            self.far.append(send(ref.at[4, :, right], ref.at[6, :, right], near(2)))
-            self.more.append(send(ref.at[4], ref.at[5], near(1)))
+            self.early.wait_recv()
+            copies = [
+                (ref.at[2, :, self.left], ref.at[6, :, self.left], near(4)),
+                (ref.at[4, :, self.right], ref.at[6, :, self.right], near(2)),
+            ]
+            self.far = send_all(copies, ref.at[6])
+
+        def to_core(self):
+            ref = self.ref
+            self.late.wait_recv()
+            self.more = [send(ref.at[r], ref.at[r + 1], near(1)) for r in (2, 4)]
 
         def diagonal(self):
-            self.far[0].wait_recv()
-            self.far[1].wait_recv()
+            self.far.wait_recv()
             self.more.append(send(self.ref.at[6], self.ref.at[7], near(1)))
 
         def chip(self, number):
-            (self.first[2] if number == 0 else self.more[number - 1]).wait_recv()
+            (self.other if number == 0 else self.more[number - 1]).wait_recv()
 
         def rows(self, number):
             return self.ref[2 * number : 2 * number + 2].reshape(256, 768)
@@ -551,8 +567,6 @@
     gather_one, gather_cot, gather_two = Gather(s.n1), Gather(s.cot), Gather(s.n2)
     pl.semaphore_wait(barrier, 10)
     gather_one.start()
-    loads["q"].start()
-    gather_cot.start()
 
     def share(source, lhs, give):
         for slot, r in enumerate(SLOTS):
@@ -564,29 +578,34 @@
     def turn_block(source, target, r):
         target[:, :, 128 * r : 128 * r + 128] = source[r].T.reshape(8, 96, 128)
 
-    turn_block(s.n1, s.n1_t, 0)
-    share_one = share(lambda at: s.n1_t[at, :, 0:128], s.lhs_q, s.give_q)
-
-    def keys_values(number):
-        rows = gather_one.rows(number)
+    def form_keys(number):
         at = 256 * number
-        s.keys[at : at + 256, :] = dot(rows, s.wqkv[:, 768:1536]).astype(LOW)
-        s.values[at : at + 256, :] = (dot(rows, s.wqkv[:, 1536:2304]) + bias_v).astype(LOW)
+        s.keys[at : at + 256, :] = dot(gather_one.rows(number), s.wqkv[:, 768:1536]).astype(LOW)
+
+    def form_values(number):
+        at = 256 * number
+        rows = dot(gather_one.rows(number), s.wqkv[:, 1536:2304]) + bias_v
+        s.values[at : at + 256, :] = rows.astype(LOW)
+
+    def active_grad(first, last):
+        for j in range(first, last):
+            rows = s.wdown[4 * j : 4 * j + 4].reshape(384, 768)
+            s.d_act[:, 384 * j : 384 * j + 384] = dot_rows(cot_ref[...], rows)
 
     loads["kv"].wait()
-    loads["down"].start()
-    loads["out"].start()
     gather_one.chip(0)
-    keys_values(0)
+    form_keys(0)
+    form_values(0)
     loads["q"].wait()
-    loads["up"].start()
-    loads["own"].start()
     q = (dot(normed_one, s.wqkv[:, 0:768]) + bias_q).astype(LOW)
     q = (q.astype(WIDE) * 0.125).astype(LOW)
     s.q_low[...] = q
+    gather_one.forward()
     s.q_turned[...] = q.T
-    gather_one.forward()
-    turn_block(s.n1, s.n1_t, 1)
+    loads["down"].wait()
+    active_grad(0, 6)
+    gather_one.to_core()
+    active_grad(6, 8)
 
     row_at = lax.broadcasted_iota(jnp.int32, (128, 128), 0)
     lane_at = lax.broadcasted_iota(jnp.int32, (128, 128), 1)
@@ -622,31 +641,27 @@
             rows = slice(128 * r, 128 * r + 128)
             s.turned[pair, :, rows] = source[rows, at : at + 128].T
 
-    for number in (0, 1, 2, 3):
-        if number:
-            gather_one.chip(number)
-            keys_values(number)
-        if number == 1:
-            gather_one.diagonal()
+    picks(0)
+    picks(1)
+    gather_one.diagonal()
+    gather_cot.start()
+    for number in (1, 2, 3):
+        gather_one.chip(number)
+        form_keys(number)
         picks(2 * number)
         picks(2 * number + 1)
-        if number:
-            turn_block(s.n1, s.n1_t, 2 * number)
-            turn_block(s.n1, s.n1_t, 2 * number + 1)
-    sum_copies = [send(s.sums.at[0], s.sums.at[r], near(r)) for r in range(1, 8)]
-
-    def active_grad(first, last):
-        for j in range(first, last):
-            rows = s.wdown[4 * j : 4 * j + 4].reshape(384, 768)
-            s.d_act[:, 384 * j : 384 * j + 384] = dot_rows(cot_ref[...], rows)
-
-    loads["down"].wait()
-    active_grad(0, 8)
-    gather_cot.forward()
+    sum_copy = send_all(
+        [(s.sums.at[0], s.sums.at[r], near(r)) for r in range(1, 8)], s.sums.at[pl.ds(1, 7)]
+    )
+    for number in (1, 2, 3):
+        form_values(number)
     for pair in range(6):
         turn(s.values, pair)
-    for copy in sum_copies:
-        copy.wait_recv()
+    gather_cot.forward()
+    for r in range(8):
+        turn_block(s.n1, s.n1_t, r)
+    share_one = share(lambda at: s.n1_t[at, :, 0:128], s.lhs_q, s.give_q)
+    sum_copy.wait_recv()
 
     def others(sums, later):
         rows = [jnp.zeros((1, 128), WIDE) for _ in range(8)]
@@ -686,8 +701,10 @@
         s.att_t[at : at + 64, :] = mixed[0:64, 0:128]
         s.att_t[at + 64 : at + 128, :] = mixed[64:128, 128:256]
 
+    gather_cot.to_core()
     for pair in range(6):
         attend(pair)
+    gather_cot.diagonal()
 
     attended_low_t = s.att_t[...].astype(LOW)
     s.att_low_t[...] = attended_low_t.reshape(8, 96, 128)
@@ -700,7 +717,6 @@
     s.n2[0] = normed_two
     gather_two.start()
     share_att = share(lambda at: s.att_low_t[at], s.lhs_out, s.give_out)
-    gather_cot.diagonal()
     loads["up"].wait()
     for j in range(4):
         at = 768 * j
@@ -711,13 +727,13 @@
         s.d_hidden[:, at : at + 768] = d_hidden
         s.wide[2 * j : 2 * j + 1, :] = column_sum(d_hidden[:, 0:384])
         s.wide[2 * j + 1 : 2 * j + 2, :] = column_sum(d_hidden[:, 384:768])
-    gather_two.forward()
 
     d_output = cot_ref[...].astype(WIDE)
     parts = []
     for j in range(3):
         parts.append(dot_rows(s.d_hidden[...], s.wup[256 * j : 256 * j + 256, :]))
     d_normed = jnp.concatenate(parts, axis=1)
+    gather_two.forward()
     unit_two = s.unit_two[...]
     s.small[5:6, :] = column_sum(d_normed * unit_two)
     s.small[6:7, :] = column_sum(d_normed)
@@ -731,7 +747,7 @@
     d_att_t = dot(s.wout[...], d_branch.T).astype(LOW)
     s.d_att_t[...] = d_att_t
     s.d_att[...] = d_att_t.T
-    gather_two.diagonal()
+    gather_two.to_core()
 
     class Unit:
         def __init__(self, rows, grads, one, two, core=None):
@@ -746,36 +762,41 @@
                 self.copy.wait_recv()
                 total = self.grads[...].astype(WIDE) + self.core[...].astype(WIDE)
                 self.grads[...] = total.astype(LOW)
-            self.copies = (
-                send(self.grads.at[pl.ds(1, 2), :, pl.ds(0, 384)], self.one.at[0], near(2)),
-                send(self.grads.at[pl.ds(2, 2), :, pl.ds(384, 384)], self.one.at[1], near(4)),
-            )
+            copies = [
+                (self.grads.at[pl.ds(1, 2), :, pl.ds(0, 384)], self.one.at[0], near(2)),
+                (self.grads.at[pl.ds(2, 2), :, pl.ds(384, 384)], self.one.at[1], near(4)),
+            ]
+            self.copy = send_all(copies, self.one)
 
         def pass_on(self):
+            self.copy.wait_recv()
             copies = []
             for half, slot, index, r in ((0, 3, 1, 4), (1, 1, 0, 2)):
                 cols = slice(384 * half, 384 * half + 384)
-                self.copies[half].wait_recv()
                 total = self.grads[slot, :, cols].astype(WIDE)
                 total = total + self.one[half, index].astype(WIDE)
                 self.grads[slot, :, cols] = total.astype(LOW)
                 source = self.grads.at[slot, :, pl.ds(384 * half, 384)]
-                copies.append(send(source, self.two.at[half], near(r)))
-            self.copies = copies
+                copies.append((source, self.two.at[half], near(r)))
+            self.copy = send_all(copies, self.two)
 
         def finish(self, half):
-            self.copies[half].wait_recv()
+            if half == 0:
+                self.copy.wait_recv()
             total = self.grads[0, :, 384 * half : 384 * half + 384].astype(WIDE)
             total = total + self.one[half, half].astype(WIDE)
             return total + self.two[half].astype(WIDE)
 
     class Line:
-        def __init__(self, at, places):
-            self.at, self.places = at, places
-            mine, total = s.mine.at[at], s.total.at[at]
-            self.inward = message(mine, s.got_z.at[at], z_pair)
-            self.across = message(mine, s.got_mid.at[at], z_middle)
-            self.outward = message(total, total, z_pair)
+        def __init__(self, at, count, places):
+            self.blocks, self.places = pl.ds(at, count), places
+            self.at = next(line_numbers)
+            send_at = RING + self.at
+            first, second = next(landings), next(landings)
+            mine, total = s.mine.at[self.blocks], s.total.at[self.blocks]
+            self.inward = message(mine, s.got_z.at[self.blocks], z_pair, send_at, first)
+            self.across = message(mine, s.got_mid.at[self.blocks], z_middle, send_at, second)
+            self.outward = message(total, total, z_pair, send_at, first)
 
         def start(self):
             pl.when(outer)(lambda: self.inward.start())
@@ -783,55 +804,66 @@
         def middle(self):
             @pl.when(inner)
             def _():
+                blocks = self.blocks
                 self.inward.wait_recv()
-                total = s.mine[self.at].astype(WIDE) + s.got_z[self.at].astype(WIDE)
-                s.mine[self.at] = total.astype(LOW)
+                total = s.mine[blocks].astype(WIDE) + s.got_z[blocks].astype(WIDE)
+                s.mine[blocks] = total.astype(LOW)
                 self.across.start()
 
         def back(self):
             @pl.when(inner)
             def _():
+                blocks = self.blocks
                 self.across.wait_recv()
-                total = s.mine[self.at].astype(WIDE) + s.got_mid[self.at].astype(WIDE)
-                s.total[self.at] = total.astype(LOW)
+                total = s.mine[blocks].astype(WIDE) + s.got_mid[blocks].astype(WIDE)
+                s.total[blocks] = total.astype(LOW)
+                self.across.wait_send()
                 self.outward.start()
 
         def write(self):
             pl.when(outer)(lambda: self.outward.wait_recv())
-            for i, where in enumerate(self.places):
-                copy = pltpu.make_async_copy(
-                    s.total.at[self.at, i], total_ref.at[where], local.at[6 + 2 * self.at + i]
-                )
-                copy.start()
-                writes.append(copy)
+            landing = local.at[6 + self.at]
+            for at, count, where in self.places:
+                pltpu.make_async_copy(
+                    s.total.at[pl.ds(at, count)], total_ref.at[pl.ds(where, count)], landing
+                ).start()
+            self.written = pltpu.make_async_copy(
+                s.total.at[self.blocks], total_ref.at[self.blocks], landing
+            )
 
         def close(self):
+            self.written.wait()
             pl.when(outer)(lambda: self.inward.wait_send())
-
-            @pl.when(inner)
-            def _():
-                self.across.wait_send()
-                self.outward.wait_send()
-
-    writes = []
-    lines = [Line(j, (2 * j, 2 * j + 1)) for j in range(5)]
-    lines += [Line(5 + j, (10 + place(2 * j), 10 + place(2 * j + 1))) for j in range(4)]
-    lines += [Line(9 + j, (18 + 2 * j, 19 + 2 * j)) for j in range(3)]
+            pl.when(inner)(lambda: self.outward.wait_send())
+
+    line_numbers = iter(range(LINES))
+
+    def plain(at, count):
+        return Line(at, count, ((at, count, at),))
+
+    def spread(r):
+        return Line(10 + r, 2, [(10 + i, 1, 10 + place(i)) for i in (r, r + 1)])
+
+    line_down = [plain(2 * j, 2) for j in range(4)]
+    line_out = plain(8, 2)
+    line_up = [spread(2 * j) for j in range(4)]
+    line_q, line_k, line_v = plain(18, 2), plain(20, 2), plain(22, 2)
+    lines = line_down + [line_out] + line_up + [line_v, line_k, line_q]
+
     unit_out = Unit(96, s.grads_out, s.one.at[0], s.two.at[0])
     unit_q = Unit(96, s.grads_q, s.one.at[1], s.two.at[1])
     unit_k = Unit(96, s.grads_k, s.one.at[2], s.two.at[2], s.core_k)
     unit_v = Unit(96, s.grads_v, s.one.at[3], s.two.at[3], s.core_v)
     unit_n1 = Unit(128, s.d_n1, s.one_n1, s.two_n1, s.core_n1)
 
-    def to_line(unit, at):
+    def to_line(unit, at, line):
         for half in range(2):
-            s.mine[at, half] = unit.finish(half).astype(LOW)
-        lines[at].start()
+            s.mine[at + half] = unit.finish(half).astype(LOW)
+        line.start()
 
     def rows_of(source, odd):
         return jnp.concatenate([source[place(r + odd)] for r in SLOTS], axis=0)
 
-    own_down = s.wdown.at[pl.ds(4 * me, 4)]
     own_bias = jnp.zeros((1, 384), WIDE)
     for j in range(8):
         own_bias = own_bias + jnp.where(me == j, 1.0, 0.0) * bias_up[:, 384 * j : 384 * j + 384]
@@ -843,36 +875,38 @@
         at = 256 * number
         hidden = dot(gather_two.rows(number), s.wup_own[...]) + own_bias
         active, slope = gelu_parts(hidden)
-        d_active = dot_rows(gather_cot.rows(number), own_down[...].reshape(384, 768))
+        d_active = dot_rows(gather_cot.rows(number), s.wdown[pl.ds(4 * me, 4)].reshape(384, 768))
         s.act_t[:, at : at + 256] = active.astype(LOW).T
         s.slope[at : at + 256, :] = (d_active * slope).astype(LOW)
         turn_block(s.n2, s.n2_t, 2 * number)
         turn_block(s.n2, s.n2_t, 2 * number + 1)
 
-    for number in range(4):
-        own_units(number)
-    share_att.wait_recv()
-    share_branch.wait_recv()
-    s.grads_out[...] = (
-        dot(s.lhs_out[...].reshape(384, 256), s.db2[...]).astype(LOW).reshape(4, 96, 768)
-    )
-    unit_out.start()
-    cot_rows = s.cot[...].reshape(1024, 768)
-    for j in range(4):
-        grads = dot(s.act_t[96 * j : 96 * j + 96, :], cot_rows).astype(LOW)
-        s.mine[j, 0] = grads[:, 0:384]
-        s.mine[j, 1] = grads[:, 384:768]
-        lines[j].start()
-    up_copies = []
-    for odd in range(2):
-        grads = dot(rows_of(s.n2_t, odd), s.slope[...]).astype(LOW).reshape(4, 96, 384)
-        for slot, r in enumerate(SLOTS):
-            if r + odd == 0:
-                s.mine[5, 0] = grads[0]
-            else:
-                s.up_give[r + odd] = grads[slot]
-                target = s.mine.at[5 + r // 2, odd]
-                up_copies.append(send(s.up_give.at[r + odd], target, near(r + odd)))
+    def out_unit():
+        share_att.wait_recv()
+        share_branch.wait_recv()
+        grads = dot(s.lhs_out[...].reshape(384, 256), s.db2[...]).astype(LOW)
+        s.grads_out[...] = grads.reshape(4, 96, 768)
+        unit_out.start()
+
+    def down_grads():
+        grads = dot(s.act_t[...], s.cot[...].reshape(1024, 768)).astype(LOW)
+        for j in range(4):
+            for i in range(2):
+                s.mine[2 * j + i] = grads[96 * j : 96 * j + 96, 384 * i : 384 * i + 384]
+        for line in line_down:
+            line.start()
+
+    def up_grads():
+        copies = []
+        for odd in range(2):
+            grads = dot(rows_of(s.n2_t, odd), s.slope[...]).astype(LOW).reshape(4, 96, 384)
+            for slot, r in enumerate(SLOTS):
+                if r + odd == 0:
+                    s.mine[10] = grads[0]
+                else:
+                    s.up_give[r + odd] = grads[slot]
+                    copies.append((s.up_give.at[r + odd], s.mine.at[10 + r + odd], near(r + odd)))
+        return copies
 
     def logit_grads(pair):
         at = 128 * pair
@@ -912,27 +946,17 @@
         value_grads(pair)
         score_grads(pair, d_logits.astype(LOW))
 
-    attend_back(5)
-    lines[0].middle()
-    attend_back(4)
-    lines[1].middle()
-    attend_back(3)
-    unit_out.pass_on()
-    lines[2].middle()
-    attend_back(2)
-    lines[0].back()
-    lines[3].middle()
-    attend_back(1)
-    d_logits = logit_grads(0)
-    s.forgot_t[...] = d_logits[:, 0:128]
-    s.second_head[...] = d_logits[:, 128:256].astype(LOW)
-    for r in range(8):
-        turned = s.d_forgot_t[128 * r : 128 * r + 128, :].T
-        s.back_sums[0, r : r + 1, :] = column_sum(turned)
-    sum_copies = [send(s.back_sums.at[0], s.back_sums.at[r], near(r)) for r in range(1, 8)]
-    value_grads(0)
-    lines[1].back()
-    to_line(unit_out, 4)
+    def back_sums():
+        d_logits = logit_grads(0)
+        s.forgot_t[...] = d_logits[:, 0:128]
+        s.second_head[...] = d_logits[:, 128:256].astype(LOW)
+        for r in range(8):
+            turned = s.d_forgot_t[128 * r : 128 * r + 128, :].T
+            s.back_sums[0, r : r + 1, :] = column_sum(turned)
+        return send_all(
+            [(s.back_sums.at[0], s.back_sums.at[r], near(r)) for r in range(1, 8)],
+            s.back_sums.at[pl.ds(1, 7)],
+        )
 
     def key_unit(unit, half):
         grads = s.dkv[:, 768 * half : 768 * half + 768]
@@ -941,81 +965,105 @@
             unit.grads[odd] = dot(rows, grads).astype(LOW).reshape(4, 96, 768)
         unit.across()
 
+    def first_pair():
+        later_rows = others(s.back_sums, True)
+        following = jnp.where(row_at > lane_at, 1.0, 0.0).astype(LOW)
+        selected = []
+        for r in range(8):
+            at = 128 * r
+            high, rest = split_low(s.d_forgot_t[at : at + 128, :])
+            later = jnp.broadcast_to(later_rows[r], (128, 128)).T
+            d_picked = -(dot(high, following) + dot(rest, following) + later)
+            selected.append(s.forgot_t[at : at + 128, :] + s.sig_t[at : at + 128, :] * d_picked)
+        first_head = jnp.concatenate(selected, axis=0).astype(LOW)
+        score_grads(0, jnp.concatenate([first_head, s.second_head[...]], axis=1))
+        for j in range(6):
+            at = 128 * j
+            d_q = (s.dq_t[at : at + 128, :] * 0.125).astype(LOW)
+            s.dq2[0:128, at : at + 128] = d_q.T
+        return send(s.dq2.at[pl.ds(0, 128)], s.dq2.at[pl.ds(128, 128)], near(1))
+
+    def query_unit():
+        grads = dot(s.lhs_q[...].reshape(384, 256), s.dq2[...]).astype(LOW)
+        s.grads_q[...] = grads.reshape(4, 96, 768)
+        unit_q.start()
+
+    def normed_part(j):
+        cols = slice(256 * j, 256 * j + 256)
+        grads = dot_rows(s.dkv[...], s.wqkv[cols, 768:2304]).astype(LOW)
+        for slot, r in enumerate(SLOTS):
+            for odd in range(2):
+                at = 128 * (r + odd)
+                s.d_n1[odd, slot, :, cols] = grads[at : at + 128]
+
+    own_units(0)
+    own_units(1)
+    own_units(2)
+    gather_two.diagonal()
+    out_unit()
+    own_units(3)
+    down_grads()
+    up_copies = up_grads()
+    up_copy = send_all(up_copies, s.up_give.at[pl.ds(1, 7)])
+    attend_back(5)
+    unit_out.pass_on()
+    attend_back(4)
+    attend_back(3)
+    attend_back(2)
+    line_down[0].middle()
+    attend_back(1)
+    sum_copy = back_sums()
+    value_grads(0)
     key_unit(unit_v, 1)
-    for copy in up_copies:
-        copy.wait_recv()
-    for j in range(4):
-        lines[5 + j].start()
-    for copy in sum_copies:
-        copy.wait_recv()
-    later_rows = others(s.back_sums, True)
-    following = jnp.where(row_at > lane_at, 1.0, 0.0).astype(LOW)
-    selected = []
-    for r in range(8):
-        at = 128 * r
-        high, rest = split_low(s.d_forgot_t[at : at + 128, :])
-        later = jnp.broadcast_to(later_rows[r], (128, 128)).T
-        d_picked = -(dot(high, following) + dot(rest, following) + later)
-        selected.append(s.forgot_t[at : at + 128, :] + s.sig_t[at : at + 128, :] * d_picked)
-    first_head = jnp.concatenate(selected, axis=0).astype(LOW)
-    score_grads(0, jnp.concatenate([first_head, s.second_head[...]], axis=1))
-    for j in range(6):
-        at = 128 * j
-        d_q = (s.dq_t[at : at + 128, :] * 0.125).astype(LOW)
-        s.dq2[0:128, at : at + 128] = d_q.T
-    share_q = send(s.dq2.at[pl.ds(0, 128)], s.dq2.at[pl.ds(128, 128)], near(1))
+    line_down[1].middle()
+    sum_copy.wait_recv()
     unit_v.start()
-    lines[2].back()
+    line_down[0].back()
+    share_q = first_pair()
+    line_down[2].middle()
+    to_line(unit_out, 8, line_out)
+    up_copy.wait_recv()
+    for line in line_up:
+        line.start()
     key_unit(unit_k, 0)
-    lines[3].back()
-    lines[4].middle()
-    lines[5].middle()
+    line_down[1].back()
     share_one.wait_recv()
     share_q.wait_recv()
-    s.grads_q[...] = (
-        dot(s.lhs_q[...].reshape(384, 256), s.dq2[...]).astype(LOW).reshape(4, 96, 768)
-    )
-    unit_q.start()
+    query_unit()
+    unit_v.pass_on()
     unit_k.start()
-    unit_v.pass_on()
-    lines[6].middle()
-    lines[4].back()
-    for slot, r in enumerate(SLOTS):
-        for odd in range(2):
-            at = 128 * (r + odd)
-            for j in range(3):
-                cols = slice(256 * j, 256 * j + 256)
-                grads = dot_rows(s.dkv[at : at + 128, :], s.wqkv[cols, 768:2304])
-                s.d_n1[odd, slot, :, cols] = grads.astype(LOW)
+    line_down[3].middle()
+    normed_part(0)
+    line_down[2].back()
+    normed_part(1)
+    line_out.middle()
+    unit_q.pass_on()
+    normed_part(2)
     unit_n1.across()
-    lines[7].middle()
-    lines[5].back()
-    unit_q.pass_on()
+    line_down[3].back()
+    to_line(unit_v, 22, line_v)
+    line_up[0].middle()
+    unit_k.pass_on()
     unit_n1.start()
-    to_line(unit_v, 11)
-    lines[8].middle()
-    lines[6].back()
-    unit_k.pass_on()
+    line_out.back()
     mixed = jnp.zeros((128, 768), WIDE)
     for j in range(4):
         rows = s.wdown[8 * j : 8 * j + 8].reshape(768, 768)
         mixed = mixed + dot(s.act[:, 768 * j : 768 * j + 768], rows)
     out_ref[...] = (s.middle[...] + mixed + bias_down).astype(LOW)
+    line_up[1].middle()
+    to_line(unit_q, 18, line_q)
+    to_line(unit_k, 20, line_k)
+    line_up[0].back()
     parts = []
     for i in range(3):
         rows = s.wqkv[256 * i : 256 * i + 256, 0:768]
         parts.append(dot_rows(s.dq2[0:128, :], rows))
     d_normed = jnp.concatenate(parts, axis=1)
-    to_line(unit_q, 9)
-    lines[11].middle()
-    lines[7].back()
     unit_n1.pass_on()
-    to_line(unit_k, 10)
-    lines[8].back()
-    lines[9].middle()
-    lines[11].back()
-    for j in (0, 1, 2, 3, 4, 5, 6):
-        lines[j].write()
+    line_up[2].middle()
+    line_up[1].back()
+    line_up[3].middle()
     d_normed = d_normed + jnp.concatenate([unit_n1.finish(0), unit_n1.finish(1)], axis=1)
     unit_one, scale_one = norm_parts(x_ref[...].astype(WIDE))
     s.small[0:1, :] = column_sum(d_normed * unit_one)
@@ -1030,30 +1078,42 @@
         s.pieces[j, 0:8, 0:96] = s.small[:, 96 * j : 96 * j + 96]
         for i in range(3):
             s.pieces[j, 8 + i : 9 + i, :] = s.wide[j : j + 1, 128 * i : 128 * i + 128]
-    piece_copies = [
-        send(s.pieces.at[place(r)], s.pieces_got.at[r], near(r)) for r in range(1, 8)
-    ]
-    lines[10].middle()
-    lines[9].back()
+    piece_copy = send_all(
+        [(s.pieces.at[place(r)], s.pieces_got.at[r], near(r)) for r in range(1, 8)],
+        s.pieces_got.at[pl.ds(1, 7)],
+    )
+    line_up[2].back()
+    line_v.middle()
+    piece_copy.wait_recv()
     total = s.pieces[me]
     for r in range(1, 8):
-        piece_copies[r - 1].wait_recv()
         total = total + s.pieces_got[r]
     s.rows_z[dp] = total
-    z_copies = [send(s.rows_z.at[dp], s.rows_z.at[dp], device) for device in others_z]
-    lines[10].back()
-    for j in (7, 8, 11, 9):
-        lines[j].write()
-    for copy in z_copies:
-        copy.wait_recv()
+    z_copy = send_all(
+        [(s.rows_z.at[dp], s.rows_z.at[dp], device) for device in others_z],
+        s.rows_z.at[pl.ds(0, 3)],
+    )
+    line_up[3].back()
+    line_q.middle()
+    for line in line_down:
+        line.write()
+    line_v.back()
+    line_k.middle()
+    line_out.write()
+    line_q.back()
+    for line in line_up:
+        line.write()
+    line_k.back()
+    line_v.write()
+    line_q.write()
+    z_copy.wait_recv()
     small_ref[...] = s.rows_z[0] + s.rows_z[1] + s.rows_z[2] + s.rows_z[3]
-    lines[10].write()
-    for copy in writes:
-        copy.wait()
-    for copy in messages:
-        copy.wait_send()
+    line_k.write()
     for line in lines:
         line.close()
+    for copy in ring:
+        if copy is not None:
+            copy.wait_send()
 
 
 def spread_kernel(total_ref, small_ref, out_in, grad_in, out_ref, grad_ref, *outs):
@@ -1112,9 +1172,9 @@
         out_specs=(vmem, vmem, anywhere, vmem),
         scratch_shapes=[pltpu.VMEM(shape, kind) for shape, kind in SCRATCH.values()]
         + [
-            pltpu.SemaphoreType.DMA((COPIES,)),
-            pltpu.SemaphoreType.DMA((COPIES,)),
-            pltpu.SemaphoreType.DMA((30,)),
+            pltpu.SemaphoreType.DMA((RING + LINES,)),
+            pltpu.SemaphoreType.DMA((LANDINGS,)),
+            pltpu.SemaphoreType.DMA((6 + LINES,)),
         ],
         compiler_params=pltpu.CompilerParams(
             collective_id=0, has_side_effects=True, vmem_limit_bytes=VMEM_BYTES

time: 112 us -> 101 us (0.902)
  Pallas kernels: 111 us -> 99.9 us
    pallas_call x1, Pallas kernels: 107 us -> 96.4 us  [fused_device(): pl.pallas_call(layer_kernel, out_shape=(jax.ShapeDtypeStruct((tokens, wid...]
where the time goes in v3:
time: 101 us
  Pallas kernels  99.9 us (99%)
    pallas_call x1, Pallas kernels, fused_device(): pl.pallas_call(layer_kernel, out_shape=(jax.ShapeDtypeStruct((tokens, wid...  96.4 us
    pallas_call x1, Pallas kernels, fused_device(): pl.pallas_call(spread_kernel, out_shape=tuple((jax.ShapeDtypeStruct((toke...  3.55 us

profile of v3, /device:TPU:0, one launch (start us, length us, event | category | flops | bytes accessed | tf_op | source)
XLA Modules:
  0.0 100.8 jit_solution(7497877032253356606)
XLA Ops:
  0.7 96.4 %layer.1 = (bf16[128,768]{1,0:T(8,128)(2,1)}, bf16[128,768]{1,0:T(8,128)(2,1)}, bf16[24,96,384]{2,1,0:T(8,128)(2,1)}, f32[16,128]{1,0:T(8,128)}) custom-call(s32[1,4]{1,0:T(1,128)} %lengths_ref.1, bf16[128,768]{1,0:T(8,128)(2,1)} %x_ref.1, bf16[128,768]{1,0:T(8,128)(2,1)} %cot_ref.1, f32[768]{0:T(1024)} %gain_one.1, f32[768]{0:T(1024)} %shift_one.1, ...), custom_call_target="tpu_custom_call" | custom-call | tf_op jit(solution)/shard_map/layer/pallas_call | solution.py:1163
  97.1 3.6 %spread.1 = (bf16[128,768]{1,0:T(8,128)(2,1)}, bf16[128,768]{1,0:T(8,128)(2,1)}, f32[96]{0:T(128)}, f32[96]{0:T(128)}, f32[96,2304]{1,0:T(8,128)}, /*index=5*/f3...) custom-call(bf16[24,96,384]{2,1,0:T(8,128)(2,1)} %get-tuple-element., ...), custom_call_target="tpu_custom_call" | custom-call | tf_op jit(solution)/shard_map/spread/pallas_call | solution.py:1184

commit v4 on v3

--- a/solution.py
+++ b/solution.py
@@ -362,7 +362,7 @@
     back_sums=((8, 8, 128), WIDE),
     forgot=((128, 1024), WIDE),
     forgot_t=((1024, 128), WIDE),
-    sig_t=((1024, 128), WIDE),
+    sig=((128, 1024), WIDE),
     d_forgot_t=((1024, 128), WIDE),
     second_head=((1024, 128), LOW),
     q_low=((128, 768), LOW),
@@ -409,11 +409,13 @@
     pieces=((8, 16, 128), WIDE),
     pieces_got=((8, 16, 128), WIDE),
     rows_z=((4, 16, 128), WIDE),
+    out=((128, 768), LOW),
+    grad=((128, 768), LOW),
 )
 SLOTS = (0, 2, 6, 4)
 RING = 24
-LINES = 12
-LANDINGS = 72
+LINES = 14
+LANDINGS = 76
 
 
 def layer_kernel(
@@ -472,6 +474,11 @@
     z_middle = (3 - dp, me)
     inner = (dp == 1) | (dp == 2)
     outer = jnp.logical_not(inner)
+    barrier = pltpu.get_barrier_semaphore()
+    others_z = [(lax.rem(dp + k, 4), me) for k in (1, 2, 3)]
+    for device in [near(r) for r in range(1, 8)] + others_z:
+        pl.semaphore_signal(barrier, inc=1, device_id=device, device_id_type=MESH)
+
     landings = iter(range(LANDINGS))
     ring = [None] * RING
     turns = iter(range(10**6))
@@ -512,11 +519,6 @@
     ):
         loads[name] = pltpu.make_async_copy(source, target, local.at[at])
         loads[name].start()
-
-    barrier = pltpu.get_barrier_semaphore()
-    others_z = [(lax.rem(dp + k, 4), me) for k in (1, 2, 3)]
-    for device in [near(r) for r in range(1, 8)] + others_z:
-        pl.semaphore_signal(barrier, inc=1, device_id=device, device_id_type=MESH)
 
     class Gather:
         def __init__(self, ref):
@@ -600,13 +602,6 @@
     q = (dot(normed_one, s.wqkv[:, 0:768]) + bias_q).astype(LOW)
     q = (q.astype(WIDE) * 0.125).astype(LOW)
     s.q_low[...] = q
-    gather_one.forward()
-    s.q_turned[...] = q.T
-    loads["down"].wait()
-    active_grad(0, 6)
-    gather_one.to_core()
-    active_grad(6, 8)
-
     row_at = lax.broadcasted_iota(jnp.int32, (128, 128), 0)
     lane_at = lax.broadcasted_iota(jnp.int32, (128, 128), 1)
     query_at = row_at + me * 128
@@ -620,20 +615,27 @@
     first_lanes = jnp.where(lane_at < 64, 1.0, 0.0)
     head_zero = (s.q_low[:, 0:128].astype(WIDE) * first_lanes).astype(LOW)
 
-    def picks(r):
-        scores = dot_rows(head_zero, s.keys[128 * r : 128 * r + 128, 0:128])
-        key_at = lane_at + place(r) * 128
-        allowed = (key_at <= query_at) & (key_at >= begin)
-        chosen = (key_at < query_at) & (key_at > begin)
+    def picks(number):
+        at = 256 * number
+        scores = dot_rows(head_zero, s.keys[at : at + 256, 0:128])
+        key_at = jnp.concatenate(
+            [lane_at + place(r) * 128 for r in (2 * number, 2 * number + 1)], axis=1
+        )
+        queries_at = jnp.concatenate([query_at, query_at], axis=1)
+        begins = jnp.concatenate([begin, begin], axis=1)
+        allowed = (key_at <= queries_at) & (key_at >= begins)
+        chosen = (key_at < queries_at) & (key_at > begins)
         small_exp = jnp.exp(-jnp.abs(scores))
         soft = jnp.maximum(scores, 0.0) + jnp.log1p(small_exp)
         picked = jnp.where(chosen, soft, 0.0) * (1.0 / 1024)
         high, rest = split_low(picked)
-        s.sums[0, r : r + 1, :] = column_sum(picked)
+        sums = column_sum(picked)
+        s.sums[0, 2 * number : 2 * number + 1, :] = sums[:, 0:128]
+        s.sums[0, 2 * number + 1 : 2 * number + 2, :] = sums[:, 128:256]
         within = dot(earlier, high) + dot(earlier, rest)
-        s.forgot[:, 128 * r : 128 * r + 128] = jnp.where(allowed, within, FAR)
+        s.forgot[:, at : at + 256] = jnp.where(allowed, within, FAR)
         sigmoid = jnp.where(scores >= 0, 1.0, small_exp) / (1.0 + small_exp)
-        s.sig_t[128 * r : 128 * r + 128, :] = (jnp.where(chosen, sigmoid, 0.0) * (1.0 / 1024)).T
+        s.sig[:, at : at + 256] = jnp.where(chosen, sigmoid, 0.0) * (1.0 / 1024)
 
     def turn(source, pair):
         at = 128 * pair
@@ -642,24 +644,27 @@
             s.turned[pair, :, rows] = source[rows, at : at + 128].T
 
     picks(0)
-    picks(1)
+    turn_block(s.n1, s.n1_t, 0)
+    gather_one.forward()
+    s.q_turned[...] = q.T
+    loads["down"].wait()
+    active_grad(0, 6)
+    gather_one.to_core()
+    active_grad(6, 8)
+
     gather_one.diagonal()
-    gather_cot.start()
     for number in (1, 2, 3):
         gather_one.chip(number)
         form_keys(number)
-        picks(2 * number)
-        picks(2 * number + 1)
+        picks(number)
     sum_copy = send_all(
         [(s.sums.at[0], s.sums.at[r], near(r)) for r in range(1, 8)], s.sums.at[pl.ds(1, 7)]
     )
+    gather_cot.start()
     for number in (1, 2, 3):
         form_values(number)
     for pair in range(6):
         turn(s.values, pair)
-    gather_cot.forward()
-    for r in range(8):
-        turn_block(s.n1, s.n1_t, r)
     share_one = share(lambda at: s.n1_t[at, :, 0:128], s.lhs_q, s.give_q)
     sum_copy.wait_recv()
 
@@ -701,10 +706,12 @@
         s.att_t[at : at + 64, :] = mixed[0:64, 0:128]
         s.att_t[at + 64 : at + 128, :] = mixed[64:128, 128:256]
 
-    gather_cot.to_core()
     for pair in range(6):
+        if pair == 2:
+            gather_cot.forward()
+        if pair == 4:
+            gather_cot.to_core()
         attend(pair)
-    gather_cot.diagonal()
 
     attended_low_t = s.att_t[...].astype(LOW)
     s.att_low_t[...] = attended_low_t.reshape(8, 96, 128)
@@ -717,6 +724,7 @@
     s.n2[0] = normed_two
     gather_two.start()
     share_att = share(lambda at: s.att_low_t[at], s.lhs_out, s.give_out)
+    gather_cot.diagonal()
     loads["up"].wait()
     for j in range(4):
         at = 768 * j
@@ -844,11 +852,11 @@
     def spread(r):
         return Line(10 + r, 2, [(10 + i, 1, 10 + place(i)) for i in (r, r + 1)])
 
-    line_down = [plain(2 * j, 2) for j in range(4)]
+    line_down = [plain(at, count) for at, count in ((0, 1), (1, 1), (2, 2), (4, 2), (6, 2))]
     line_out = plain(8, 2)
     line_up = [spread(2 * j) for j in range(4)]
-    line_q, line_k, line_v = plain(18, 2), plain(20, 2), plain(22, 2)
-    lines = line_down + [line_out] + line_up + [line_v, line_k, line_q]
+    line_v, line_q, line_k = plain(22, 2), plain(18, 2), [plain(20, 1), plain(21, 1)]
+    lines = line_down + [line_out] + line_up + [line_v, line_q] + line_k
 
     unit_out = Unit(96, s.grads_out, s.one.at[0], s.two.at[0])
     unit_q = Unit(96, s.grads_q, s.one.at[1], s.two.at[1])
@@ -856,10 +864,11 @@
     unit_v = Unit(96, s.grads_v, s.one.at[3], s.two.at[3], s.core_v)
     unit_n1 = Unit(128, s.d_n1, s.one_n1, s.two_n1, s.core_n1)
 
-    def to_line(unit, at, line):
+    def to_line(unit, at, *parts):
         for half in range(2):
             s.mine[at + half] = unit.finish(half).astype(LOW)
-        line.start()
+        for line in parts:
+            line.start()
 
     def rows_of(source, odd):
         return jnp.concatenate([source[place(r + odd)] for r in SLOTS], axis=0)
@@ -878,8 +887,6 @@
         d_active = dot_rows(gather_cot.rows(number), s.wdown[pl.ds(4 * me, 4)].reshape(384, 768))
         s.act_t[:, at : at + 256] = active.astype(LOW).T
         s.slope[at : at + 256, :] = (d_active * slope).astype(LOW)
-        turn_block(s.n2, s.n2_t, 2 * number)
-        turn_block(s.n2, s.n2_t, 2 * number + 1)
 
     def out_unit():
         share_att.wait_recv()
@@ -896,17 +903,16 @@
         for line in line_down:
             line.start()
 
-    def up_grads():
+    def up_grads(odd):
         copies = []
-        for odd in range(2):
-            grads = dot(rows_of(s.n2_t, odd), s.slope[...]).astype(LOW).reshape(4, 96, 384)
-            for slot, r in enumerate(SLOTS):
-                if r + odd == 0:
-                    s.mine[10] = grads[0]
-                else:
-                    s.up_give[r + odd] = grads[slot]
-                    copies.append((s.up_give.at[r + odd], s.mine.at[10 + r + odd], near(r + odd)))
-        return copies
+        grads = dot(rows_of(s.n2_t, odd), s.slope[...]).astype(LOW).reshape(4, 96, 384)
+        for slot, r in enumerate(SLOTS):
+            if r + odd == 0:
+                s.mine[10] = grads[0]
+            else:
+                s.up_give[r + odd] = grads[slot]
+                copies.append((s.up_give.at[r + odd], s.mine.at[10 + r + odd], near(r + odd)))
+        return copies, s.up_give.at[pl.ds(0, len(copies))]
 
     def logit_grads(pair):
         at = 128 * pair
@@ -958,12 +964,10 @@
             s.back_sums.at[pl.ds(1, 7)],
         )
 
-    def key_unit(unit, half):
+    def key_unit(unit, half, odd):
         grads = s.dkv[:, 768 * half : 768 * half + 768]
-        for odd in (1, 0):
-            rows = rows_of(s.n1_t, odd)
-            unit.grads[odd] = dot(rows, grads).astype(LOW).reshape(4, 96, 768)
-        unit.across()
+        rows = rows_of(s.n1_t, odd)
+        unit.grads[odd] = dot(rows, grads).astype(LOW).reshape(4, 96, 768)
 
     def first_pair():
         later_rows = others(s.back_sums, True)
@@ -974,7 +978,7 @@
             high, rest = split_low(s.d_forgot_t[at : at + 128, :])
             later = jnp.broadcast_to(later_rows[r], (128, 128)).T
             d_picked = -(dot(high, following) + dot(rest, following) + later)
-            selected.append(s.forgot_t[at : at + 128, :] + s.sig_t[at : at + 128, :] * d_picked)
+            selected.append(s.forgot_t[at : at + 128, :] + s.sig[:, at : at + 128].T * d_picked)
         first_head = jnp.concatenate(selected, axis=0).astype(LOW)
         score_grads(0, jnp.concatenate([first_head, s.second_head[...]], axis=1))
         for j in range(6):
@@ -1003,67 +1007,84 @@
     out_unit()
     own_units(3)
     down_grads()
-    up_copies = up_grads()
-    up_copy = send_all(up_copies, s.up_give.at[pl.ds(1, 7)])
+    for r in range(8):
+        turn_block(s.n2, s.n2_t, r)
+        if r:
+            turn_block(s.n1, s.n1_t, r)
+    up_odd = send_all(*up_grads(1))
+    up_even = up_grads(0)
     attend_back(5)
+    attend_back(4)
     unit_out.pass_on()
-    attend_back(4)
     attend_back(3)
+    line_down[0].middle()
     attend_back(2)
-    line_down[0].middle()
+    line_down[1].middle()
+    line_down[0].back()
     attend_back(1)
     sum_copy = back_sums()
+    up_even = send_all(*up_even)
     value_grads(0)
-    key_unit(unit_v, 1)
-    line_down[1].middle()
+    key_unit(unit_v, 1, 1)
+    line_down[2].middle()
+    key_unit(unit_v, 1, 0)
+    unit_v.across()
+    line_down[1].back()
+    to_line(unit_out, 8, line_out)
     sum_copy.wait_recv()
+    share_q = first_pair()
     unit_v.start()
-    line_down[0].back()
-    share_q = first_pair()
-    line_down[2].middle()
-    to_line(unit_out, 8, line_out)
-    up_copy.wait_recv()
-    for line in line_up:
-        line.start()
-    key_unit(unit_k, 0)
-    line_down[1].back()
+    line_down[3].middle()
+    line_down[2].back()
+    key_unit(unit_k, 0, 1)
+    key_unit(unit_k, 0, 0)
+    unit_k.across()
     share_one.wait_recv()
     share_q.wait_recv()
     query_unit()
+    up_odd.wait_recv()
+    up_even.wait_recv()
+    for line in line_up:
+        line.start()
+    line_down[4].middle()
+    line_down[3].back()
+    normed_part(0)
     unit_v.pass_on()
     unit_k.start()
-    line_down[3].middle()
-    normed_part(0)
-    line_down[2].back()
+    line_out.middle()
+    line_down[4].back()
     normed_part(1)
-    line_out.middle()
-    unit_q.pass_on()
     normed_part(2)
     unit_n1.across()
-    line_down[3].back()
+    unit_q.pass_on()
+    line_up[0].middle()
+    line_out.back()
     to_line(unit_v, 22, line_v)
-    line_up[0].middle()
-    unit_k.pass_on()
-    unit_n1.start()
-    line_out.back()
     mixed = jnp.zeros((128, 768), WIDE)
     for j in range(4):
         rows = s.wdown[8 * j : 8 * j + 8].reshape(768, 768)
         mixed = mixed + dot(s.act[:, 768 * j : 768 * j + 768], rows)
-    out_ref[...] = (s.middle[...] + mixed + bias_down).astype(LOW)
+    s.out[...] = (s.middle[...] + mixed + bias_down).astype(LOW)
+    out_copy = pltpu.make_async_copy(s.out, out_ref, local.at[6 + LINES])
+    out_copy.start()
+    unit_k.pass_on()
+    unit_n1.start()
     line_up[1].middle()
+    line_up[0].back()
     to_line(unit_q, 18, line_q)
-    to_line(unit_k, 20, line_k)
-    line_up[0].back()
+    line_up[2].middle()
+    to_line(unit_k, 20, *line_k)
+    line_up[1].back()
     parts = []
     for i in range(3):
         rows = s.wqkv[256 * i : 256 * i + 256, 0:768]
         parts.append(dot_rows(s.dq2[0:128, :], rows))
     d_normed = jnp.concatenate(parts, axis=1)
+    line_up[3].middle()
+    line_up[2].back()
     unit_n1.pass_on()
-    line_up[2].middle()
-    line_up[1].back()
-    line_up[3].middle()
+    line_v.middle()
+    line_up[3].back()
     d_normed = d_normed + jnp.concatenate([unit_n1.finish(0), unit_n1.finish(1)], axis=1)
     unit_one, scale_one = norm_parts(x_ref[...].astype(WIDE))
     s.small[0:1, :] = column_sum(d_normed * unit_one)
@@ -1071,7 +1092,9 @@
     s.small[2:3, :] = column_sum(s.dq2[0:128, :])
     s.small[3:4, :] = column_sum(s.dkv[:, 768:1536])
     d_inputs = s.d_mid[...] + norm_back(d_normed, unit_one, scale_one, gain_one)
-    grad_ref[...] = d_inputs.astype(LOW)
+    s.grad[...] = d_inputs.astype(LOW)
+    grad_copy = pltpu.make_async_copy(s.grad, grad_ref, local.at[7 + LINES])
+    grad_copy.start()
 
     s.pieces[...] = jnp.zeros((8, 16, 128), WIDE)
     for j in range(8):
@@ -1082,8 +1105,11 @@
         [(s.pieces.at[place(r)], s.pieces_got.at[r], near(r)) for r in range(1, 8)],
         s.pieces_got.at[pl.ds(1, 7)],
     )
-    line_up[2].back()
-    line_v.middle()
+    line_q.middle()
+    line_v.back()
+    line_k[0].middle()
+    line_k[1].middle()
+    line_q.back()
     piece_copy.wait_recv()
     total = s.pieces[me]
     for r in range(1, 8):
@@ -1093,22 +1119,18 @@
         [(s.rows_z.at[dp], s.rows_z.at[dp], device) for device in others_z],
         s.rows_z.at[pl.ds(0, 3)],
     )
-    line_up[3].back()
-    line_q.middle()
-    for line in line_down:
+    line_k[0].back()
+    line_k[1].back()
+    for line in line_down + [line_out] + line_up:
         line.write()
-    line_v.back()
-    line_k.middle()
-    line_out.write()
-    line_q.back()
-    for line in line_up:
-        line.write()
-    line_k.back()
     line_v.write()
     line_q.write()
     z_copy.wait_recv()
     small_ref[...] = s.rows_z[0] + s.rows_z[1] + s.rows_z[2] + s.rows_z[3]
-    line_k.write()
+    for line in line_k:
+        line.write()
+    out_copy.wait()
+    grad_copy.wait()
     for line in lines:
         line.close()
     for copy in ring:
@@ -1169,12 +1191,12 @@
             jax.ShapeDtypeStruct((16, 128), WIDE),
         ),
         in_specs=[pl.BlockSpec(memory_space=pltpu.SMEM)] + [vmem] * 11 + [anywhere] * 4,
-        out_specs=(vmem, vmem, anywhere, vmem),
+        out_specs=(anywhere, anywhere, anywhere, vmem),
         scratch_shapes=[pltpu.VMEM(shape, kind) for shape, kind in SCRATCH.values()]
         + [
             pltpu.SemaphoreType.DMA((RING + LINES,)),
             pltpu.SemaphoreType.DMA((LANDINGS,)),
-            pltpu.SemaphoreType.DMA((6 + LINES,)),
+            pltpu.SemaphoreType.DMA((8 + LINES,)),
         ],
         compiler_params=pltpu.CompilerParams(
             collective_id=0, has_side_effects=True, vmem_limit_bytes=VMEM_BYTES

time: 101 us -> 97.7 us (0.967)
  Pallas kernels: 99.9 us -> 96.7 us
    pallas_call x1, Pallas kernels: 96.4 us -> 93.2 us  [fused_device(): pl.pallas_call(layer_kernel, out_shape=(jax.ShapeDtypeStruct((tokens, wid...]
where the time goes in v4:
time: 97.7 us; the launch traced here: 97.6 us
  Pallas kernels  96.7 us (99%)
    pallas_call x1, Pallas kernels, fused_device(): pl.pallas_call(layer_kernel, out_shape=(jax.ShapeDtypeStruct((tokens, wid...  93.2 us
    pallas_call x1, Pallas kernels, fused_device(): pl.pallas_call(spread_kernel, out_shape=tuple((jax.ShapeDtypeStruct((toke...  3.55 us

profile of v4, /device:TPU:0, one launch (start us, length us, event | category | flops | bytes accessed | tf_op | source)
XLA Modules:
  0.0 97.6 jit_solution(14244349567396391691)
XLA Ops:
  0.7 93.2 %layer.1 = (bf16[128,768]{1,0:T(8,128)(2,1)}, bf16[128,768]{1,0:T(8,128)(2,1)}, bf16[24,96,384]{2,1,0:T(8,128)(2,1)}, f32[16,128]{1,0:T(8,128)}) custom-call(s32[1,4]{1,0:T(1,128)} %lengths_ref.1, bf16[128,768]{1,0:T(8,128)(2,1)} %x_ref.1, bf16[128,768]{1,0:T(8,128)(2,1)} %cot_ref.1, f32[768]{0:T(1024)} %gain_one.1, f32[768]{0:T(1024)} %shift_one.1, ...), custom_call_target="tpu_custom_call" | custom-call | tf_op jit(solution)/shard_map/layer/pallas_call | solution.py:1185
  93.8 3.6 %spread.1 = (bf16[128,768]{1,0:T(8,128)(2,1)}, bf16[128,768]{1,0:T(8,128)(2,1)}, f32[96]{0:T(128)}, f32[96]{0:T(128)}, f32[96,2304]{1,0:T(8,128)}, /*index=5*/f3...) custom-call(bf16[24,96,384]{2,1,0:T(8,128)(2,1)} %get-tuple-element., ...), custom_call_target="tpu_custom_call" | custom-call | tf_op jit(solution)/shard_map/spread/pallas_call | solution.py:1206

commit v5 on v4

--- a/solution.py
+++ b/solution.py
@@ -414,8 +414,8 @@
 )
 SLOTS = (0, 2, 6, 4)
 RING = 24
-LINES = 14
-LANDINGS = 76
+LINES = 15
+LANDINGS = 78
 
 
 def layer_kernel(
@@ -796,8 +796,8 @@
             return total + self.two[half].astype(WIDE)
 
     class Line:
-        def __init__(self, at, count, places):
-            self.blocks, self.places = pl.ds(at, count), places
+        def __init__(self, blocks, places):
+            self.blocks, self.places = blocks, places
             self.at = next(line_numbers)
             send_at = RING + self.at
             first, second = next(landings), next(landings)
@@ -831,9 +831,9 @@
         def write(self):
             pl.when(outer)(lambda: self.outward.wait_recv())
             landing = local.at[6 + self.at]
-            for at, count, where in self.places:
+            for source, target in self.places:
                 pltpu.make_async_copy(
-                    s.total.at[pl.ds(at, count)], total_ref.at[pl.ds(where, count)], landing
+                    s.total.at[source], total_ref.at[target], landing
                 ).start()
             self.written = pltpu.make_async_copy(
                 s.total.at[self.blocks], total_ref.at[self.blocks], landing
@@ -847,15 +847,21 @@
     line_numbers = iter(range(LINES))
 
     def plain(at, count):
-        return Line(at, count, ((at, count, at),))
+        blocks = (pl.ds(at, count),)
+        return Line(blocks, ((blocks, blocks),))
+
+    def part(at, first):
+        blocks = (at, pl.ds(first, 48))
+        return Line(blocks, ((blocks, blocks),))
 
     def spread(r):
-        return Line(10 + r, 2, [(10 + i, 1, 10 + place(i)) for i in (r, r + 1)])
+        return Line((pl.ds(10 + r, 2),), [(10 + i, 10 + place(i)) for i in (r, r + 1)])
 
     line_down = [plain(at, count) for at, count in ((0, 1), (1, 1), (2, 2), (4, 2), (6, 2))]
     line_out = plain(8, 2)
     line_up = [spread(2 * j) for j in range(4)]
-    line_v, line_q, line_k = plain(22, 2), plain(18, 2), [plain(20, 1), plain(21, 1)]
+    line_v, line_q = plain(22, 2), plain(18, 2)
+    line_k = [plain(20, 1), part(21, 0), part(21, 48)]
     lines = line_down + [line_out] + line_up + [line_v, line_q] + line_k
 
     unit_out = Unit(96, s.grads_out, s.one.at[0], s.two.at[0])
@@ -895,12 +901,14 @@
         s.grads_out[...] = grads.reshape(4, 96, 768)
         unit_out.start()
 
-    def down_grads():
-        grads = dot(s.act_t[...], s.cot[...].reshape(1024, 768)).astype(LOW)
-        for j in range(4):
+    def down_grads(half, parts):
+        rows = s.act_t[192 * half : 192 * half + 192, :]
+        grads = dot(rows, s.cot[...].reshape(1024, 768)).astype(LOW)
+        for j in range(2):
             for i in range(2):
-                s.mine[2 * j + i] = grads[96 * j : 96 * j + 96, 384 * i : 384 * i + 384]
-        for line in line_down:
+                block = grads[96 * j : 96 * j + 96, 384 * i : 384 * i + 384]
+                s.mine[4 * half + 2 * j + i] = block
+        for line in parts:
             line.start()
 
     def up_grads(odd):
@@ -1006,7 +1014,8 @@
     gather_two.diagonal()
     out_unit()
     own_units(3)
-    down_grads()
+    down_grads(0, line_down[0:3])
+    down_grads(1, line_down[3:5])
     for r in range(8):
         turn_block(s.n2, s.n2_t, r)
         if r:
@@ -1016,14 +1025,14 @@
     attend_back(5)
     attend_back(4)
     unit_out.pass_on()
+    line_down[0].middle()
     attend_back(3)
-    line_down[0].middle()
     attend_back(2)
     line_down[1].middle()
-    line_down[0].back()
     attend_back(1)
     sum_copy = back_sums()
     up_even = send_all(*up_even)
+    line_down[0].back()
     value_grads(0)
     key_unit(unit_v, 1, 1)
     line_down[2].middle()
@@ -1109,6 +1118,7 @@
     line_v.back()
     line_k[0].middle()
     line_k[1].middle()
+    line_k[2].middle()
     line_q.back()
     piece_copy.wait_recv()
     total = s.pieces[me]
@@ -1121,6 +1131,7 @@
     )
     line_k[0].back()
     line_k[1].back()
+    line_k[2].back()
     for line in line_down + [line_out] + line_up:
         line.write()
     line_v.write()

time: 97.7 us -> 96.2 us (0.985)
  Pallas kernels: 96.7 us -> 95.2 us
    pallas_call x1, Pallas kernels: 93.2 us -> 91.6 us  [fused_device(): pl.pallas_call(layer_kernel, out_shape=(jax.ShapeDtypeStruct((tokens, wid...]
where the time goes in v5:
time: 96.2 us; the launch traced here: 96 us
  Pallas kernels  95.2 us (99%)
    pallas_call x1, Pallas kernels, fused_device(): pl.pallas_call(layer_kernel, out_shape=(jax.ShapeDtypeStruct((tokens, wid...  91.6 us
    pallas_call x1, Pallas kernels, fused_device(): pl.pallas_call(spread_kernel, out_shape=tuple((jax.ShapeDtypeStruct((toke...  3.55 us

profile of v5, /device:TPU:0, one launch (start us, length us, event | category | flops | bytes accessed | tf_op | source)
XLA Modules:
  0.0 96.0 jit_solution(16904461589072077605)
XLA Ops:
  0.7 91.6 %layer.1 = (bf16[128,768]{1,0:T(8,128)(2,1)}, bf16[128,768]{1,0:T(8,128)(2,1)}, bf16[24,96,384]{2,1,0:T(8,128)(2,1)}, f32[16,128]{1,0:T(8,128)}) custom-call(s32[1,4]{1,0:T(1,128)} %lengths_ref.1, bf16[128,768]{1,0:T(8,128)(2,1)} %x_ref.1, bf16[128,768]{1,0:T(8,128)(2,1)} %cot_ref.1, f32[768]{0:T(1024)} %gain_one.1, f32[768]{0:T(1024)} %shift_one.1, ...), custom_call_target="tpu_custom_call" | custom-call | tf_op jit(solution)/shard_map/layer/pallas_call | solution.py:1196
  92.3 3.6 %spread.1 = (bf16[128,768]{1,0:T(8,128)(2,1)}, bf16[128,768]{1,0:T(8,128)(2,1)}, f32[96]{0:T(128)}, f32[96]{0:T(128)}, f32[96,2304]{1,0:T(8,128)}, /*index=5*/f3...) custom-call(bf16[24,96,384]{2,1,0:T(8,128)(2,1)} %get-tuple-element., ...), custom_call_target="tpu_custom_call" | custom-call | tf_op jit(solution)/shard_map/spread/pallas_call | solution.py:1217

commit v6 on v5

--- a/solution.py
+++ b/solution.py
@@ -1048,6 +1048,8 @@
     key_unit(unit_k, 0, 1)
     key_unit(unit_k, 0, 0)
     unit_k.across()
+    line_down[4].middle()
+    line_down[3].back()
     share_one.wait_recv()
     share_q.wait_recv()
     query_unit()
@@ -1055,8 +1057,6 @@
     up_even.wait_recv()
     for line in line_up:
         line.start()
-    line_down[4].middle()
-    line_down[3].back()
     normed_part(0)
     unit_v.pass_on()
     unit_k.start()
@@ -1076,10 +1076,10 @@
     s.out[...] = (s.middle[...] + mixed + bias_down).astype(LOW)
     out_copy = pltpu.make_async_copy(s.out, out_ref, local.at[6 + LINES])
     out_copy.start()
+    line_up[1].middle()
+    line_up[0].back()
     unit_k.pass_on()
     unit_n1.start()
-    line_up[1].middle()
-    line_up[0].back()
     to_line(unit_q, 18, line_q)
     line_up[2].middle()
     to_line(unit_k, 20, *line_k)

time: 96.2 us -> 97.8 us (1.017)
  Pallas kernels: 95.2 us -> 96.8 us
    pallas_call x1, Pallas kernels: 91.6 us -> 93.3 us  [fused_device(): pl.pallas_call(layer_kernel, out_shape=(jax.ShapeDtypeStruct((tokens, wid...]
where the time goes in v6:
time: 97.8 us; the launch traced here: 97.7 us
  Pallas kernels  96.8 us (99%)
    pallas_call x1, Pallas kernels, fused_device(): pl.pallas_call(layer_kernel, out_shape=(jax.ShapeDtypeStruct((tokens, wid...  93.3 us
    pallas_call x1, Pallas kernels, fused_device(): pl.pallas_call(spread_kernel, out_shape=tuple((jax.ShapeDtypeStruct((toke...  3.55 us

profile of v6, /device:TPU:0, one launch (start us, length us, event | category | flops | bytes accessed | tf_op | source)
XLA Modules:
  0.0 97.7 jit_solution(5095843917584234692)
XLA Ops:
  0.7 93.3 %layer.1 = (bf16[128,768]{1,0:T(8,128)(2,1)}, bf16[128,768]{1,0:T(8,128)(2,1)}, bf16[24,96,384]{2,1,0:T(8,128)(2,1)}, f32[16,128]{1,0:T(8,128)}) custom-call(s32[1,4]{1,0:T(1,128)} %lengths_ref.1, bf16[128,768]{1,0:T(8,128)(2,1)} %x_ref.1, bf16[128,768]{1,0:T(8,128)(2,1)} %cot_ref.1, f32[768]{0:T(1024)} %gain_one.1, f32[768]{0:T(1024)} %shift_one.1, ...), custom_call_target="tpu_custom_call" | custom-call | tf_op jit(solution)/shard_map/layer/pallas_call | solution.py:1196
  93.9 3.6 %spread.1 = (bf16[128,768]{1,0:T(8,128)(2,1)}, bf16[128,768]{1,0:T(8,128)(2,1)}, f32[96]{0:T(128)}, f32[96]{0:T(128)}, f32[96,2304]{1,0:T(8,128)}, /*index=5*/f3...) custom-call(bf16[24,96,384]{2,1,0:T(8,128)(2,1)} %get-tuple-element., ...), custom_call_target="tpu_custom_call" | custom-call | tf_op jit(solution)/shard_map/spread/pallas_call | solution.py:1217
